TPU v7x, 256 devices: a whole 4x4x8 slice. The times are simulated.
256 devices in a mesh: batch: 32 (over x, z_lo, core), field: 8 (over z_hi, y).
Axes of the slice: x: 4, y: 4, z: 8 (z_hi: 2, z_lo: 4; z = z_hi * 4 + z_lo), core: 2. Of those that a mesh axis runs over, the one named last changes fastest.
Arguments:
- embeddings: bfloat16 [4096, 768, 192], P('batch', 'field'), may hold values from -6 to 6
- compress: bfloat16 [768, 16], P('field'), may hold values from -0.21875 to 0.21875
- w_up: bfloat16 [1024, 12288], P(None, 'field'), may hold values from -0.0546875 to 0.0546875
- up_bias: float32 [1024], replicated, may hold values from -3 to 3
- w_down: bfloat16 [1024, 9216], P(None, 'field'), may hold values from -0.1875 to 0.1875
- w_linear: bfloat16 [768, 96], P('field'), may hold values from -0.21875 to 0.21875
- ln_gain: float32 [192], replicated, may hold values from 0.5 to 1.5
- cot_fm: bfloat16 [4096, 48, 192], P('batch', 'field'), may hold values from -0.09375 to 0.09375
- cot_lc: bfloat16 [4096, 96, 192], P('batch', 'field'), may hold values from -0.09375 to 0.09375
Outputs:
- fm_out: bfloat16 [4096, 48, 192], P('batch', 'field')
- lc_out: bfloat16 [4096, 96, 192], P('batch', 'field')
- grad_compress: float32 [768, 16], P('field')
- grad_up: float32 [1024, 12288], P('batch', 'field')
- grad_bias: float32 [1024], replicated
- grad_down: float32 [1024, 9216], P('batch', 'field')
- grad_linear: float32 [768, 96], P('field')
- grad_gain: float32 [192], replicated
All inputs are finite; a program needn't handle non-finite values.
Results may differ from a plain program's by a relative error of at most 0.012.
Values may be sent and summed in bfloat16 or wider, within the bound.
A program may use at most 128 MiB of HBM per device.

v0:
```python
import jax
import jax.numpy as jnp
from jax import lax
from jax.sharding import PartitionSpec as P


def norm_rows(values):
    centre = values - jnp.mean(values, axis=-1, keepdims=True)
    rstd = lax.rsqrt(jnp.mean(centre * centre, axis=-1, keepdims=True) + 1e-05)
    return (centre * rstd, rstd)


def norm_back(cotangent, normed, rstd, ln_gain):
    dn = cotangent * ln_gain
    return rstd * (
        dn
        - jnp.mean(dn, axis=-1, keepdims=True)
        - normed * jnp.mean(dn * normed, axis=-1, keepdims=True)
    )


def local(embeddings, compress, w_up, up_bias, w_down, w_linear, ln_gain, cot_fm, cot_lc):
    examples, local_fields, width = embeddings.shape
    inv_root = jnp.float32(width) ** (-0.5)
    comp_partial = jnp.einsum(
        "bfe,fk->bke", embeddings, compress, preferred_element_type=jnp.float32
    )
    linear_partial = jnp.einsum(
        "bfe,fn->bne", embeddings, w_linear, preferred_element_type=jnp.float32
    )
    compressed = lax.psum(comp_partial, "field").astype(jnp.bfloat16)
    lc_raw = lax.psum_scatter(linear_partial, "field", scatter_dimension=1, tiled=True)
    interact = (
        jnp.einsum("bfe,bke->bfk", embeddings, compressed, preferred_element_type=jnp.float32)
        * inv_root
    ).astype(jnp.bfloat16)
    flat = interact.reshape(examples, -1)
    pre_partial = jnp.einsum("bj,hj->bh", flat, w_up, preferred_element_type=jnp.float32)
    hidden_pre = lax.psum(pre_partial, "field") + up_bias
    hidden = jax.nn.silu(hidden_pre).astype(jnp.bfloat16)
    fm_raw = jnp.dot(hidden, w_down, preferred_element_type=jnp.float32).reshape(
        examples, -1, width
    )
    fm_normed, fm_rstd = norm_rows(fm_raw)
    lc_normed, lc_rstd = norm_rows(lc_raw)
    fm_out = (fm_normed * ln_gain).astype(jnp.bfloat16)
    lc_out = (lc_normed * ln_gain).astype(jnp.bfloat16)
    cot_first = cot_fm.astype(jnp.float32)
    cot_second = cot_lc.astype(jnp.float32)
    gain_local = jnp.sum(cot_first * fm_normed, axis=(0, 1)) + jnp.sum(
        cot_second * lc_normed, axis=(0, 1)
    )
    grad_fm = (
        norm_back(cot_first, fm_normed, fm_rstd, ln_gain).astype(jnp.bfloat16).reshape(examples, -1)
    )
    grad_lc = norm_back(cot_second, lc_normed, lc_rstd, ln_gain).astype(jnp.bfloat16)
    grad_down = lax.psum_scatter(
        jnp.einsum("bh,bc->hc", hidden, grad_fm, preferred_element_type=jnp.float32),
        "batch",
        scatter_dimension=0,
        tiled=True,
    )
    hidden_partial = jnp.einsum("bc,hc->bh", grad_fm, w_down, preferred_element_type=jnp.float32)
    grad_hidden = lax.psum(hidden_partial, "field")
    sigma = jax.nn.sigmoid(hidden_pre)
    grad_pre32 = grad_hidden * sigma * (1.0 + hidden_pre * (1.0 - sigma))
    bias_local = jnp.sum(grad_pre32, axis=0)
    grad_pre = grad_pre32.astype(jnp.bfloat16)
    grad_up = lax.psum_scatter(
        jnp.einsum("bh,bj->hj", grad_pre, flat, preferred_element_type=jnp.float32),
        "batch",
        scatter_dimension=0,
        tiled=True,
    )
    grad_inter = (
        jnp.dot(grad_pre, w_up, preferred_element_type=jnp.float32)
        .astype(jnp.bfloat16)
        .reshape(examples, local_fields, -1)
    )
    comp_back = jnp.einsum(
        "bfk,bfe->bke", grad_inter, embeddings, preferred_element_type=jnp.float32
    )
    grad_comp = (lax.psum(comp_back, "field") * inv_root).astype(jnp.bfloat16)
    comp_local = jnp.einsum(
        "bfe,bke->fk", embeddings, grad_comp, preferred_element_type=jnp.float32
    )
    linear_local = jnp.einsum(
        "bfe,bne->fn",
        embeddings,
        lax.all_gather(grad_lc, "field", axis=1, tiled=True),
        preferred_element_type=jnp.float32,
    )
    grad_compress, grad_linear, grad_bias = lax.psum(
        (comp_local, linear_local, bias_local), "batch"
    )
    grad_gain = lax.psum(gain_local, ("batch", "field"))
    return (fm_out, lc_out, grad_compress, grad_up, grad_bias, grad_down, grad_linear, grad_gain)


def solution(mesh):
    placed = (
        P("batch", "field", None),
        P("field", None),
        P(None, "field"),
        P(),
        P(None, "field"),
        P("field", None),
        P(),
        P("batch", "field", None),
        P("batch", "field", None),
    )
    return jax.shard_map(
        local,
        mesh=mesh,
        in_specs=placed,
        out_specs=(
            P("batch", "field", None),
            P("batch", "field", None),
            P("field", None),
            P("batch", "field"),
            P(),
            P("batch", "field"),
            P("field", None),
            P(),
        ),
        check_vma=False,
    )
```

profile of v0, /device:TPU:1, one launch (start us, length us, event | category | flops | bytes accessed | tf_op | source)
XLA Modules:
  0.0 1125.4 jit_solution(18214340478120817599)
XLA Ops:
  7.2 9.3 copy.52
  16.5 5.1 convolution_bitcast_fusion
  21.6 116.2 %all-reduce.11 = bf16[128,16,192]{2,1,0:T(8,128)(2,1)} all-reduce(f32[128,16,192]{2,1,0:T(8,128)} %convolution_bitcast_fusion), channel_id=1, replica_groups=mesh['batch'=32,'field'=8] {'field'}, use_global_device_ids=true, to_apply=%region_0.0 | all-reduce | flops 393216 | bytes 2359296 | tf_op jit(solution)/shard_map/psum | solution.py:31
  137.8 5.7 fusion.14
  143.5 1.7 copy.54
  145.2 2.0 fusion.46
  147.2 105.5 %all-reduce.6.cloned.1.call-done = f32[128,1024]{1,0:T(8,128)} async-done(((f32[128,1024]{1,0:T(8,128)}), f32[128,1024]{1,0:T(8,128)}) %all-reduce.6.cloned.1.call-update) | async-done | bytes 524304 | tf_op jit(solution)/shard_map/psum | solution.py:39
  252.8 3.7 fusion.44
  260.3 2.1 fusion.35
  263.2 1.7 fusion.47
  265.1 5.8 fusion.7
  271.0 9.1 copy.58
  280.1 89.2 %all-reduce.8.cloned.1.call-done = f32[128,1024]{1,0:T(8,128)} async-done(((f32[128,1024]{1,0:T(8,128)}), f32[128,1024]{1,0:T(8,128)}) %all-reduce.8.cloned.1.call-update) | async-done | bytes 524304 | tf_op jit(solution)/shard_map/psum | solution.py:64
  373.9 3.7 fusion.48
  377.6 1.8 copy.62
  379.8 195.8 %reduce-scatter.4.cloned.1.call-done = f32[128,12,192]{0,2,1:T(8,128)} async-done(((f32[128,96,192]{0,2,1:T(8,128)}), f32[128,12,192]{0,2,1:T(8,128)}) %reduce-scatter.4.cloned.1.call-update) | async-done | bytes 1179664 | tf_op jit(solution)/shard_map/reduce_scatter | solution.py:32
  580.8 3.0 fusion.43
  584.8 3.7 fusion.38
  588.5 104.9 %all-reduce.10.cloned.1.call-done = f32[128,16,192]{0,2,1:T(8,128)} async-done(((f32[128,16,192]{0,2,1:T(8,128)}), f32[128,16,192]{0,2,1:T(8,128)}) %all-reduce.10.cloned.1.call-update) | async-done | bytes 1572880 | tf_op jit(solution)/shard_map/psum | solution.py:83
  695.0 5.3 fusion.25
  700.3 121.6 %psum.63 = f32[192]{0:T(256)} all-reduce(f32[192]{0:T(256)S(1)} %add.71), channel_id=1, replica_groups=mesh['batch'=32,'field'=8] {'batch','field'}, use_global_device_ids=true, to_apply=%region_21.22 | all-reduce | flops 192 | bytes 1536 | tf_op jit(solution)/shard_map/psum | solution.py:96
  821.9 9.0 fusion.20
  830.9 129.2 %all-reduce = (f32[96,16]{0,1:T(8,128)}, f32[1024]{0:T(1024)}, f32[96,96]{0,1:T(8,128)S(1)}) all-reduce(f32[96,16]{0,1:T(8,128)S(1)} %fusion.25, f32[1024]{0:T(1024)S(1)} %get-tuple-element.49, f32[96,96]{0,1:T(8,128)S(1)} %fusion.20), channel_id=1, replica_groups=mesh['batch'=32,'field'=8] {'batch'}, use_global_device_ids=true, to_apply=%region_11.12 | all-reduce | flops 11776 | bytes 94208 | tf_op jit(solution)/shard_map/psum | solution.py:93
  961.3 157.3 %reduce-scatter.6.cloned.1.call-done = f32[32,1536]{1,0:T(8,128)} async-done(((f32[1024,1536]{1,0:T(8,128)}), f32[32,1536]{1,0:T(8,128)}) %reduce-scatter.6.cloned.1.call-update) | async-done | bytes 196624 | tf_op jit(solution)/shard_map/reduce_scatter | solution.py:69
  (64 shorter events, 18.7 us)
Async XLA Ops:
  7.2 138.0 %copy-start = (bf16[1024,1536]{1,0:T(8,128)(2,1)S(1)}, bf16[1024,1536]{1,0:T(8,128)(2,1)}, u32[]{:S(2)}) copy-start(bf16[1024,1536]{1,0:T(8,128)(2,1)} %param.11) | copy-start | bytes 9437188
  7.2 9.3 copy-start.13
  7.2 245.6 %all-reduce.6.cloned.1.call-start = ((), (), s32[]{:S(2)}) async-start(), calls=%async_computation.3 | async-start | bytes 1048576 | tf_op jit(solution)/shard_map/psum | solution.py:39
  145.2 111.3 %copy-start.3 = (bf16[128,96,16]{0,2,1:T(8,128)(2,1)}, bf16[128,96,16]{0,2,1:T(8,128)(2,1)S(1)}, u32[]{:S(2)}) copy-start(bf16[128,96,16]{0,2,1:T(8,128)(2,1)S(1)} %copy.54) | copy-start | bytes 1179652
  145.2 107.6 %copy-start.11 = (f32[1024]{0:T(1024)S(1)}, f32[1024]{0:T(1024)}, u32[]{:S(2)}) copy-start(f32[1024]{0:T(1024)} %param.12) | copy-start | bytes 12292
  147.2 111.7 %copy-start.12 = (f32[192]{0:T(256)S(1)}, f32[192]{0:T(256)}, u32[]{:S(2)}) copy-start(f32[192]{0:T(256)} %param.15) | copy-start | bytes 2308
  147.2 222.1 %all-reduce.8.cloned.1.call-start = ((), (), s32[]{:S(2)}) async-start(), calls=%async_computation.5 | async-start | bytes 1048576 | tf_op jit(solution)/shard_map/psum | solution.py:64
  257.6 5.6 copy-start.7
  260.3 4.8 copy-start.10
  262.5 0.7 copy-start.5
  264.9 310.7 %reduce-scatter.4.cloned.1.call-start = ((), (), s32[]{:S(2)}) async-start(), calls=%async_computation.4 | async-start | bytes 10616832 | tf_op jit(solution)/shard_map/reduce_scatter | solution.py:32
  280.1 413.3 %all-reduce.10.cloned.1.call-start = ((), (), s32[]{:S(2)}) async-start(), calls=%async_computation.6 | async-start | bytes 3145728 | tf_op jit(solution)/shard_map/psum | solution.py:83
  379.5 199.0 %copy-start.8 = (bf16[128,12,192]{0,2,1:T(8,128)(2,1)S(1)}, bf16[128,12,192]{0,2,1:T(8,128)(2,1)}, u32[]{:S(2)}) copy-start(bf16[128,12,192]{0,2,1:T(8,128)(2,1)} %param.17) | copy-start | bytes 1769476
  379.5 442.4 %all-gather.2.cloned.1.call-start = ((), (), s32[]{:S(2)}) async-start(), calls=%async_computation.9 | async-start | bytes 5308416 | tf_op jit(solution)/shard_map/all_gather | solution.py:90
  575.6 2.9 copy-start.2
  578.5 2.2 copy-start.6
  578.5 2.2 copy-start.9
  580.7 380.6 %reduce-scatter.8.cloned.1.call-start = ((), (), s32[]{:S(2)}) async-start(), calls=%async_computation.8 | async-start | bytes 4866048 | tf_op jit(solution)/shard_map/reduce_scatter | solution.py:57
  583.8 1.0 copy-start.4
  583.8 534.7 %reduce-scatter.6.cloned.1.call-start = ((), (), s32[]{:S(2)}) async-start(), calls=%async_computation.7 | async-start | bytes 6488064 | tf_op jit(solution)/shard_map/reduce_scatter | solution.py:69
  821.9 296.7 %copy-start.1 = (bf16[1024,1536]{1,0:T(8,128)(2,1)S(1)}, bf16[1024,1536]{1,0:T(8,128)(2,1)}, u32[]{:S(2)}) copy-start(bf16[1024,1536]{1,0:T(8,128)(2,1)} %param.11) | copy-start | bytes 9437188
Sparse Core Ops, SparseCore 0:
  147.3 105.4 all-reduce.5
  265.0 104.2 all-reduce.7
  373.5 202.0 reduce-scatter.3
  578.3 114.9 all-reduce.9
  696.2 115.5 all-gather.1
  814.8 146.4 reduce-scatter.7
  964.6 153.9 reduce-scatter.5
where the time goes:
time: 1130 us
  waiting for transfers between devices  653 us (58%)
  blocking collectives  367 us (32%)
  matrix products  49.9 us (4%)
  local copies, waits for them, and re-layouts  26.1 us (2%)
  between operations  14.4 us (1%)
  other arithmetic  14 us (1%)
    reduce_scatter x1, waiting for transfers between devices, local(): lax.psum_scatter(linear_partial, 'field', scatter_dimension=1, tiled=True)  196 us
    reduce_scatter x1, waiting for transfers between devices, local(): lax.psum_scatter(jnp.einsum('bh,bj->hj', grad_pre, flat, preferred_elemen...  157 us
    psum x1, blocking collectives, local(): lax.psum((comp_local, linear_local, bias_local), 'batch')  129 us
    psum x1, blocking collectives, local(): grad_gain = lax.psum(gain_local, ('batch', 'field'))  122 us
    psum x1, blocking collectives, local(): compressed = lax.psum(comp_partial, 'field').astype(jnp.bfloat16)  116 us
    psum x1, waiting for transfers between devices, local(): hidden_pre = lax.psum(pre_partial, 'field') + up_bias  106 us
    psum x1, waiting for transfers between devices, local(): grad_comp = (lax.psum(comp_back, 'field') * inv_root).astype(jnp.bfloat16)  105 us
    psum x1, waiting for transfers between devices, local(): grad_hidden = lax.psum(hidden_partial, 'field')  89.2 us
  transfers between devices with their start and end apart: 7, of which 6 were waited for; matrix products, arithmetic and copies ran while one was open for 5% of the time, Pallas kernels for 0%

commit v1 on v0

v1 whole, which is shorter than its diff:
```python
import functools

import jax
import jax.numpy as jnp
from jax import lax
from jax.experimental import pallas as pl
from jax.experimental.pallas import tpu as pltpu
from jax.sharding import PartitionSpec as P

MESH = pl.DeviceIdType.MESH
VMEM = pltpu.VMEM
F32 = jnp.float32
BF16 = jnp.bfloat16
LIMIT = 48 * 1024 * 1024


class Place:
    def __init__(self):
        batch, field = lax.axis_index("batch"), lax.axis_index("field")
        self.batch, self.field = batch, field
        self.y, self.zh = lax.rem(field, 4), lax.div(field, 4)
        self.core = lax.rem(batch, 2)
        self.zl = lax.rem(lax.div(batch, 2), 4)
        self.x = lax.div(batch, 8)

    def to_y(self, k):
        other = lax.rem(self.y + k, 4)
        return other, (self.batch, self.zh * 4 + other)

    def to_zh(self):
        other = 1 - self.zh
        return other, (self.batch, other * 4 + self.y)

    def to_core(self):
        other = 1 - self.core
        return other, (self.x * 8 + self.zl * 2 + other, self.field)

    def to_x(self, k):
        other = lax.rem(self.x + k, 4)
        return other, (other * 8 + self.zl * 2 + self.core, self.field)

    def to_zl(self, k):
        other = lax.rem(self.zl + k, 4)
        return other, (self.x * 8 + other * 2 + self.core, self.field)

    def y_group(self):
        return [self.to_y(k)[1] for k in (1, 2, 3)]

    def field_group(self):
        return self.y_group() + [self.to_zh()[1]]

    def batch_group(self):
        return [self.to_core()[1]] + [self.to_x(k)[1] for k in (1, 2, 3)] + [self.to_zl(k)[1] for k in (1, 2, 3)]


def greet(peers):
    barrier = pltpu.get_barrier_semaphore()
    for peer in peers:
        pl.semaphore_signal(barrier, inc=1, device_id=peer, device_id_type=MESH)
    pl.semaphore_wait(barrier, len(peers))


def send(src, dst, sems, index, peer):
    copy = pltpu.make_async_remote_copy(
        src_ref=src,
        dst_ref=dst,
        send_sem=sems.at[0, index],
        recv_sem=sems.at[1, index],
        device_id=peer,
        device_id_type=MESH,
    )
    copy.start()
    return copy


def params(collective_id):
    return pltpu.CompilerParams(
        collective_id=collective_id, has_side_effects=True, vmem_limit_bytes=LIMIT
    )


def cost(us):
    return pl.CostEstimate(flops=0, bytes_accessed=int(us * 3.0e6), transcendentals=0)


def call(kernel, outs, scratch, collective_id, us, *args):
    return pl.pallas_call(
        kernel,
        out_shape=[jax.ShapeDtypeStruct(shape, dtype) for shape, dtype in outs],
        in_specs=[pl.BlockSpec(memory_space=VMEM)] * len(args),
        out_specs=[pl.BlockSpec(memory_space=VMEM)] * len(outs),
        scratch_shapes=scratch,
        compiler_params=params(collective_id),
        cost_estimate=cost(us),
    )(*args)


def rows(start, size):
    return pl.ds(pl.multiple_of(start * size, size), size)


def compress_kernel(part_ref, wl_ref, out_ref, wl_out, got, mine, other, sems):
    at = Place()
    greet(at.field_group())
    step = part_ref.shape[0] // 4
    copies, sends = [], []
    for k in (1, 2, 3):
        y, peer = at.to_y(k)
        copies.append(send(part_ref.at[rows(y, step)], got.at[k - 1], sems, k - 1, peer))
    for k in (1, 2, 3):
        peer = at.to_y(k)[1]
        sends.append(send(wl_ref, wl_out.at[k - 1], sems, 2 + k, peer))
    for copy in copies:
        copy.wait()
    own = rows(at.y, step)
    mine[...] = (
        part_ref[own].astype(F32) + got[0].astype(F32) + got[1].astype(F32) + got[2].astype(F32)
    ).astype(BF16)
    send(mine, other, sems, 6, at.to_zh()[1]).wait()
    out_ref[own] = (mine[...].astype(F32) + other[...].astype(F32)).astype(BF16)
    for k in (1, 2, 3):
        sends.append(send(out_ref.at[own], out_ref.at[own], sems, 6 + k, at.to_y(k)[1]))
    for copy in sends:
        copy.wait()


def reduce_rows(at, part_ref, got, mine, other, sems):
    step = part_ref.shape[0] // 4
    copies = []
    for k in (1, 2, 3):
        y, peer = at.to_y(k)
        copies.append(send(part_ref.at[rows(y, step)], got.at[k - 1], sems, k - 1, peer))
    for copy in copies:
        copy.wait()
    mine[...] = (
        part_ref[rows(at.y, step)].astype(F32)
        + got[0].astype(F32)
        + got[1].astype(F32)
        + got[2].astype(F32)
    ).astype(BF16)
    send(mine, other, sems, 3, at.to_zh()[1]).wait()
    return mine[...].astype(F32) + other[...].astype(F32)


def gather_rows(at, out_ref, sems):
    own = rows(at.y, out_ref.shape[0] // 4)
    return [send(out_ref.at[own], out_ref.at[own], sems, 3 + k, at.to_y(k)[1]) for k in (1, 2, 3)]


def hidden_kernel(part_ref, bias_ref, hidden_ref, pre_ref, got, mine, other, sems):
    at = Place()
    greet(at.field_group())
    pre = reduce_rows(at, part_ref, got, mine, other, sems) + bias_ref[...]
    pre_ref[...] = pre
    step = part_ref.shape[0] // 4
    hidden_ref[rows(at.y, step)] = (pre / (1.0 + jnp.exp(-pre))).astype(BF16)
    for copy in gather_rows(at, hidden_ref, sems):
        copy.wait()


def back_kernel(
    part_ref, pre_ref, lin_ref, grad_ref, bias_ref, raw_ref, got, mine, other, lmine, lother, sems, lsems
):
    at = Place()
    greet(at.field_group())
    half, fields = lin_ref.shape[0] // 2, raw_ref.shape[0]
    width = lin_ref.shape[1]
    zh, zpeer = at.to_zh()
    lcopies = []
    for j in range(4):
        lcopies.append(
            send(
                lin_ref.at[pl.ds(zh * half + j * fields, fields)],
                lother.at[pl.ds(j * fields, fields)],
                lsems,
                j,
                zpeer,
            )
        )
    total = reduce_rows(at, part_ref, got, mine, other, sems)
    pre = pre_ref[...]
    sigma = 1.0 / (1.0 + jnp.exp(-pre))
    grad = total * sigma * (1.0 + pre * (1.0 - sigma))
    bias_ref[...] = jnp.sum(grad.reshape(-1, 8, grad.shape[-1]), axis=0)
    step = part_ref.shape[0] // 4
    grad_ref[rows(at.y, step)] = grad.astype(BF16)
    sends = gather_rows(at, grad_ref, sems)
    for copy in lcopies:
        copy.wait()
    columns = rows(at.y, width)
    for n in range(half):
        lmine[n] = (lin_ref[at.zh * half + n].astype(F32) + lother[n].astype(F32)).astype(BF16)
    for k in (1, 2, 3):
        y, peer = at.to_y(k)
        sends.append(
            send(lmine.at[pl.ds(y * fields, fields)], raw_ref.at[:, columns, :], lsems, 3 + k, peer)
        )
    raw_ref[:, columns, :] = lmine[pl.ds(at.y * fields, fields)]
    for copy in sends:
        copy.wait()


def grads_kernel(
    scale,
    down_ref,
    up_ref,
    glc_ref,
    cb_ref,
    gather_ref,
    down_out,
    up_out,
    cgot,
    cmine,
    cother,
    d1,
    d2,
    d3,
    u1,
    u2,
    u3,
    ysems,
    zsems,
    csems,
    dsems,
    usems,
):
    at = Place()
    greet(at.field_group() + at.batch_group())
    fields, step = glc_ref.shape[0], gather_ref.shape[1]
    kk = cb_ref.shape[0]
    half = 4 * fields
    zpeer = at.to_zh()[1]
    zbase = at.zh * half
    sends = []
    weights = ((down_ref, d1, d2, d3, dsems, down_out), (up_ref, u1, u2, u3, usems, up_out))
    firsts = []
    core, cpeer = at.to_core()
    for ref, one, two, three, sems, out in weights:
        firsts.append(send(ref.at[:, core], one, sems, 0, cpeer))
    ccopies = []
    for k in (1, 2, 3):
        y, peer = at.to_y(k)
        ccopies.append(send(cb_ref.at[:, rows(y, step), :], cgot.at[k - 1], csems, k - 1, peer))
    gcopies = []
    for k in (1, 2, 3):
        y, peer = at.to_y(k)
        gcopies.append(
            send(
                glc_ref.at[:, rows(y, step), :],
                gather_ref.at[pl.ds(zbase + at.y * fields, fields)],
                ysems,
                k - 1,
                peer,
            )
        )
    own = pl.ds(zbase + at.y * fields, fields)
    gather_ref[own] = glc_ref[:, rows(at.y, step), :]
    zcopies = [send(gather_ref.at[own], gather_ref.at[own], zsems, 0, zpeer)]
    seconds = []
    for (ref, one, two, three, sems, out), first in zip(weights, firsts):
        first.wait()
        for j in range(16):
            one[j] = (one[j].astype(F32) + ref[j, at.core].astype(F32)).astype(BF16)
        group = []
        for k in (1, 2, 3):
            x, peer = at.to_x(k)
            group.append(send(one.at[pl.ds(x * 4, 4)], two.at[k - 1], sems, k, peer))
        seconds.append(group)
    for copy in ccopies:
        copy.wait()
    cmine[...] = (
        cb_ref[:, rows(at.y, step), :].astype(F32)
        + cgot[0].astype(F32)
        + cgot[1].astype(F32)
        + cgot[2].astype(F32)
    ).astype(BF16)
    ccopy = send(cmine, cother, csems, 3, zpeer)
    for k in (1, 2, 3):
        gcopies[k - 1].wait()
        source = lax.rem(at.y + 4 - k, 4)
        part = pl.ds(zbase + source * fields, fields)
        zcopies.append(send(gather_ref.at[part], gather_ref.at[part], zsems, k, zpeer))
    ccopy.wait()
    gather_ref[pl.ds(2 * half, kk)] = (
        (cmine[...].astype(F32) + cother[...].astype(F32)) * scale
    ).astype(BF16)
    thirds = []
    for (ref, one, two, three, sems, out), group in zip(weights, seconds):
        for copy in group:
            copy.wait()
        for j in range(4):
            total = one[at.x * 4 + j].astype(F32)
            for k in range(3):
                total = total + two[k, j].astype(F32)
            two[0, j] = total.astype(BF16)
        group = []
        for k in (1, 2, 3):
            z, peer = at.to_zl(k)
            group.append(send(two.at[0, z], three.at[k - 1], sems, 3 + k, peer))
        thirds.append(group)
    for (ref, one, two, three, sems, out), group in zip(weights, thirds):
        for copy in group:
            copy.wait()
        total = two[0, at.zl].astype(F32)
        for k in range(3):
            total = total + three[k].astype(F32)
        out[...] = total
    for copy in zcopies:
        copy.wait()


def small_kernel(part_ref, rows_ref, out_ref, ygot, rgot, rmine, rother, one, xmine, xgot, zmine, zgot, sems):
    at = Place()
    greet(at.field_group() + at.batch_group())
    fields, lanes = part_ref.shape[1:]
    copies = []
    for k in (1, 2, 3):
        peer = at.to_y(4 - k)[1]
        copies.append(send(part_ref.at[k], ygot.at[k - 1], sems, k - 1, peer))
        copies.append(send(rows_ref, rgot.at[k - 1], sems, 2 + k, peer))
    for copy in copies:
        copy.wait()
    rmine[...] = (rows_ref[...] + rgot[1]) + (rgot[0] + rgot[2])
    copy = send(rmine, rother, sems, 6, at.to_zh()[1])
    one[0, :fields] = part_ref[0] + ygot[0] + ygot[1] + ygot[2]
    copy.wait()
    one[0, fields:] = rmine[...] + rother[...]
    send(one.at[0], one.at[1], sems, 7, at.to_core()[1]).wait()
    xmine[...] = one[0] + one[1]
    copies = [send(xmine, xgot.at[k - 1], sems, 7 + k, at.to_x(k)[1]) for k in (1, 2, 3)]
    for copy in copies:
        copy.wait()
    zmine[...] = (xmine[...] + xgot[1]) + (xgot[0] + xgot[2])
    copies = [send(zmine, zgot.at[k - 1], sems, 10 + k, at.to_zl(k)[1]) for k in (1, 2, 3)]
    for copy in copies:
        copy.wait()
    out_ref[...] = (zmine[...] + zgot[1]) + (zgot[0] + zgot[2])


def norm_rows(values):
    centre = values - jnp.mean(values, axis=-1, keepdims=True)
    rstd = lax.rsqrt(jnp.mean(centre * centre, axis=-1, keepdims=True) + 1e-05)
    return (centre * rstd, rstd)


def norm_back(cotangent, normed, rstd, ln_gain):
    dn = cotangent * ln_gain
    return rstd * (
        dn
        - jnp.mean(dn, axis=-1, keepdims=True)
        - normed * jnp.mean(dn * normed, axis=-1, keepdims=True)
    )


def y_shift(k):
    return [
        (b * 8 + zh * 4 + y, b * 8 + zh * 4 + (y + k) % 4)
        for b in range(32)
        for zh in range(2)
        for y in range(4)
    ]


def local(embeddings, compress, w_up, up_bias, w_down, w_linear, ln_gain, cot_fm, cot_lc):
    examples, local_fields, width = embeddings.shape
    hidden_units, kk, nl = w_up.shape[0], compress.shape[1], w_linear.shape[1]
    part = width // 4
    quarter = examples // 4
    inv_root = float(width) ** (-0.5)
    y = lax.rem(lax.axis_index("field"), 4)
    turned = embeddings.transpose(1, 2, 0)

    slices = []
    for k in (0, 1, 2, 3):
        piece = lax.dynamic_slice_in_dim(turned, lax.rem(y + k, 4) * part, part, axis=1)
        slices.append(piece if k == 0 else lax.ppermute(piece, ("batch", "field"), y_shift(k)))

    comp_part = jnp.einsum("feb,fk->ekb", turned, compress, preferred_element_type=F32).astype(BF16)
    wl = jnp.pad(w_linear, ((0, 0), (0, 128 - nl)))
    compressed, wl_got = call(
        compress_kernel,
        [(comp_part.shape, BF16), ((3, local_fields, 128), BF16)],
        [
            VMEM((3, part, kk, examples), BF16),
            VMEM((part, kk, examples), BF16),
            VMEM((part, kk, examples), BF16),
            pltpu.SemaphoreType.DMA((2, 10)),
        ],
        0,
        30,
        comp_part,
        wl,
    )
    interact = (
        jnp.einsum("bfe,ekb->bfk", embeddings, compressed, preferred_element_type=F32) * inv_root
    ).astype(BF16)
    flat = interact.reshape(examples, -1)
    pre_part = jnp.einsum("bj,hj->bh", flat, w_up, preferred_element_type=F32).astype(BF16)
    row_scratch = [
        VMEM((3, quarter, hidden_units), BF16),
        VMEM((quarter, hidden_units), BF16),
        VMEM((quarter, hidden_units), BF16),
    ]
    hidden, hidden_pre = call(
        hidden_kernel,
        [((examples, hidden_units), BF16), ((quarter, hidden_units), F32)],
        row_scratch + [pltpu.SemaphoreType.DMA((2, 7))],
        1,
        15,
        pre_part,
        up_bias.reshape(1, -1),
    )
    fm_raw = jnp.dot(hidden, w_down, preferred_element_type=F32).reshape(examples, -1, width)
    fm_normed, fm_rstd = norm_rows(fm_raw)
    fm_out = (fm_normed * ln_gain).astype(BF16)
    cot_first = cot_fm.astype(F32)
    gain_local = jnp.sum(cot_first * fm_normed, axis=(0, 1))
    grad_fm = norm_back(cot_first, fm_normed, fm_rstd, ln_gain).astype(BF16).reshape(examples, -1)
    hidden_part = jnp.einsum("bc,hc->bh", grad_fm, w_down, preferred_element_type=F32).astype(BF16)

    lin = sum(
        jnp.einsum(
            "feb,fn->neb",
            slices[k],
            w_linear if k == 0 else wl_got[k - 1, :, :nl],
            preferred_element_type=F32,
        )
        for k in range(4)
    ).astype(BF16)
    out_fields = nl // 8
    grad_pre, bias_part, lc_raw = call(
        back_kernel,
        [
            ((examples, hidden_units), BF16),
            ((8, hidden_units), F32),
            ((out_fields, width, examples), BF16),
        ],
        row_scratch
        + [
            VMEM((nl // 2, part, examples), BF16),
            VMEM((nl // 2, part, examples), BF16),
            pltpu.SemaphoreType.DMA((2, 7)),
            pltpu.SemaphoreType.DMA((2, 7)),
        ],
        2,
        35,
        hidden_part,
        hidden_pre,
        lin,
    )
    lc_raw = lc_raw.transpose(2, 0, 1).astype(F32)
    lc_normed, lc_rstd = norm_rows(lc_raw)
    lc_out = (lc_normed * ln_gain).astype(BF16)
    cot_second = cot_lc.astype(F32)
    gain_local = gain_local + jnp.sum(cot_second * lc_normed, axis=(0, 1))
    grad_lc = norm_back(cot_second, lc_normed, lc_rstd, ln_gain).astype(BF16)

    down_part = jnp.einsum("bh,bc->hc", hidden, grad_fm, preferred_element_type=F32).astype(BF16)
    up_part = jnp.einsum("bh,bj->hj", grad_pre, flat, preferred_element_type=F32).astype(BF16)
    grad_inter = (
        jnp.dot(grad_pre, w_up, preferred_element_type=F32)
        .astype(BF16)
        .reshape(examples, local_fields, -1)
    )
    comp_back = jnp.einsum(
        "bfk,bfe->keb", grad_inter, embeddings, preferred_element_type=F32
    ).astype(BF16)
    own_rows = hidden_units // 32
    down_columns, up_columns = w_down.shape[1], w_up.shape[1]

    def stages(columns):
        return [
            VMEM((16, own_rows, columns), BF16),
            VMEM((3, 4, own_rows, columns), BF16),
            VMEM((3, own_rows, columns), BF16),
        ]

    gathered, grad_down, grad_up = call(
        functools.partial(grads_kernel, inv_root),
        [
            ((nl + kk, part, examples), BF16),
            ((own_rows, down_columns), F32),
            ((own_rows, up_columns), F32),
        ],
        [
            VMEM((3, kk, part, examples), BF16),
            VMEM((kk, part, examples), BF16),
            VMEM((kk, part, examples), BF16),
        ]
        + stages(down_columns)
        + stages(up_columns)
        + [
            pltpu.SemaphoreType.DMA((2, 3)),
            pltpu.SemaphoreType.DMA((2, 4)),
            pltpu.SemaphoreType.DMA((2, 4)),
            pltpu.SemaphoreType.DMA((2, 7)),
            pltpu.SemaphoreType.DMA((2, 7)),
        ],
        3,
        60,
        down_part.reshape(16, 2, own_rows, down_columns),
        up_part.reshape(16, 2, own_rows, up_columns),
        grad_lc.transpose(1, 2, 0),
        comp_back,
    )
    mixed = jnp.stack(
        [
            jnp.einsum("feb,neb->fn", slices[k], gathered, preferred_element_type=F32)
            for k in range(4)
        ]
    )
    mixed = jnp.pad(mixed, ((0, 0), (0, 0), (0, 128 - nl - kk)))
    bias_rows = 0.5 * jnp.sum(bias_part, axis=0).reshape(-1, 128)
    gain_rows = jnp.pad(gain_local, (0, 256 - width)).reshape(-1, 128)
    extra = jnp.concatenate([bias_rows, gain_rows])
    n_extra = 16
    extra = jnp.pad(extra, ((0, n_extra - extra.shape[0]), (0, 0)))
    total_rows = local_fields + n_extra
    (sums,) = call(
        small_kernel,
        [((total_rows, 128), F32)],
        [
            VMEM((3, local_fields, 128), F32),
            VMEM((3, n_extra, 128), F32),
            VMEM((n_extra, 128), F32),
            VMEM((n_extra, 128), F32),
            VMEM((2, total_rows, 128), F32),
            VMEM((total_rows, 128), F32),
            VMEM((3, total_rows, 128), F32),
            VMEM((total_rows, 128), F32),
            VMEM((3, total_rows, 128), F32),
            pltpu.SemaphoreType.DMA((2, 14)),
        ],
        4,
        20,
        mixed,
        extra,
    )
    grad_linear = sums[:local_fields, :nl]
    grad_compress = sums[:local_fields, nl : nl + kk]
    n_bias = hidden_units // 128
    grad_bias = sums[local_fields : local_fields + n_bias].reshape(-1)
    grad_gain = sums[local_fields + n_bias : local_fields + n_bias + 2].reshape(-1)[:width]
    return (fm_out, lc_out, grad_compress, grad_up, grad_bias, grad_down, grad_linear, grad_gain)


def solution(mesh):
    placed = (
        P("batch", "field", None),
        P("field", None),
        P(None, "field"),
        P(),
        P(None, "field"),
        P("field", None),
        P(),
        P("batch", "field", None),
        P("batch", "field", None),
    )
    return jax.shard_map(
        local,
        mesh=mesh,
        in_specs=placed,
        out_specs=(
            P("batch", "field", None),
            P("batch", "field", None),
            P("field", None),
            P("batch", "field"),
            P(),
            P("batch", "field"),
            P("field", None),
            P(),
        ),
        check_vma=False,
    )
```

time: 1130 us -> 299 us (0.26)
  waiting for transfers between devices: 653 us -> 0.01 us
  blocking collectives: 367 us -> 0 us
  Pallas kernels: 0 us -> 203 us
  between operations: 14.4 us -> 1.11 us
  matrix products: 49.9 us -> 37.6 us
    psum x3 -> x0, blocking collectives: 367 us -> none  [the longest x1 129 us: local(): lax.psum((comp_local, linear_local, bias_local), 'batch')]
    reduce_scatter x3 -> x0, waiting for transfers between devices: 354 us -> none  [the longest x1 196 us: local(): lax.psum_scatter(linear_partial, 'field', scatter_dimension=1, tiled=True)]
    psum x3 -> x0, waiting for transfers between devices: 300 us -> none  [the longest x1 106 us: local(): hidden_pre = lax.psum(pre_partial, 'field') + up_bias]
    pallas_call x0 -> x5, Pallas kernels: none -> 203 us  [call(): pl.pallas_call(kernel, out_shape=[jax.ShapeDtypeStruct(shape, dtype) for...]
    dot_general x12 -> x17, matrix products: 49.9 us -> 37.6 us  [the longest x4 5.99 us: local(): jnp.einsum('feb,neb->fn', slices[k], gathered, preferred_element_type=F32)]
  transfers between devices with their start and end apart: 7 -> 3, of which waited for: 6 -> 0; matrix products, arithmetic and copies ran while one was open for 5% -> 14% of each run, Pallas kernels for 0% -> 26%
where the time goes in v1:
time: 299 us; the launch traced here: 298 us
  Pallas kernels  203 us (68%)
  matrix products  37.6 us (13%)
  local copies, waits for them, and re-layouts  35.7 us (12%)
  other arithmetic  15.9 us (5%)
  starting transfers between devices  4.6 us (2%)
    pallas_call x5, Pallas kernels, call(): pl.pallas_call(kernel, out_shape=[jax.ShapeDtypeStruct(shape, dtype) for...  203 us
    unnamed x59, local copies, waits for them, and re-layouts  19.1 us
    dot_general x4, matrix products, local(): jnp.einsum('feb,neb->fn', slices[k], gathered, preferred_element_type=F32)  5.99 us
  transfers between devices with their start and end apart: 3, of which 0 were waited for; matrix products, arithmetic and copies ran while one was open for 14% of the time, Pallas kernels for 26%

profile of v1, /device:TPU:1, one launch (start us, length us, event | category | flops | bytes accessed | tf_op | source)
XLA Modules:
  0.0 297.7 jit_solution(13855823709887229078)
XLA Ops:
  0.7 4.4 %constant_dynamic-slice_fusion.3 = (bf16[128,96,48]{0,2,1:T(8,128)(2,1)}, bf16[128,96,48]{0,2,1:T(8,128)(2,1)S(1)}, bf16[128,96,48]{0,2,1:T(8,128)(2,1)S(1)}, bf16[128,96,48]{0,2,1:T(8,128)(2,1)S(1)}) fusion(bf16[128,96,192]{0,2,1:T(8,128)(2,1)} %param.9, s32[]{:T(128)S(6)} %select_n.12, s32[]{:T(128)S(6)} %select_n.14, s32[]{:T(128)S(6)} %select_n.13, ...), kind=kLoop, calls=%fused_computation.94 | loop fusion | bytes 9437200 | tf_op jit(solution)/shard_map/dynamic-slice
  6.4 3.6 %collective-permute-start.2 = (bf16[96,48,128]{2,0,1:T(8,128)(2,1)}, bf16[96,48,128]{2,0,1:T(8,128)(2,1)}, u32[]{:S(2)}, u32[]{:S(2)}) collective-permute-start(bf16[96,48,128]{2,0,1:T(8,128)(2,1)} %bitcast.121), channel_id=1, source_target_pairs={{0,3},{1,0},{2,1},{3,2},{4,7},{5,4},{6,5},{7,6},{8,11},{9,8},{10,9... | collective-permute-start | bytes 3538952 | tf_op jit(solution)/shard_map/ppermute | solution.py:376
  13.8 9.0 %copy.43 = bf16[128,96,192]{2,1,0:T(8,128)(2,1)} copy(bf16[128,96,192]{0,2,1:T(8,128)(2,1)} %param.9) | data formatting | bytes 9437184 | tf_op args[0]
  22.8 5.0 %fusion.12.part_ref = bf16[192,16,128]{2,1,0:T(8,128)(2,1)S(1)} fusion(bf16[96,192,128]{2,1,0:T(8,128)(2,1)} %bitcast.128, bf16[96,16]{0,1:T(8,128)(2,1)S(1)} %copy-done.24), kind=kOutput, calls=%fused_computation.17 | convolution fusion | flops 75890688 | bytes 5508096 | tf_op jit(solution)/shard_map/feb,fk->ekb/dot_general | solution.py:378
  27.9 62.1 %shard_map.152 = (bf16[192,16,128]{2,1,0:T(8,128)(2,1)S(1)}, bf16[3,96,128]{2,1,0:T(8,128)(2,1)S(1)}) custom-call(bf16[192,16,128]{2,1,0:T(8,128)(2,1)S(1)} %fusion.12.part_ref, bf16[96,128]{1,0:T(8,128)(2,1)S(1)} %pad.16.wl_ref), custom_call_target="tpu_custom_call" | custom-call | bytes 90000000 | tf_op jit(solution)/shard_map/pallas_call | solution.py:87
  91.5 2.9 copy.42
  94.3 5.7 %fusion.15 = bf16[128,96,16]{1,2,0:T(8,128)(2,1)} fusion(bf16[192,16,128]{0,1,2:T(8,128)(2,1)} %copy.42, bf16[128,96,192]{2,1,0:T(8,128)(2,1)} %copy.43), kind=kOutput, calls=%fused_computation.18 | convolution fusion | flops 75890688 | bytes 5898240 | tf_op jit(solution)/shard_map/bfe,ekb->bfk/dot_general | solution.py:395
  102.9 15.1 %shard_map.153 = (bf16[128,1024]{1,0:T(8,128)(2,1)S(1)}, f32[32,1024]{1,0:T(8,128)S(1)}) custom-call(bf16[128,1024]{1,0:T(8,128)(2,1)S(1)} %convolution_convert_fusion.4.part_ref, f32[1,1024]{1,0:T(1,128)S(1)} %bitcast.127), custom_call_target="tpu_custom_call" | custom-call | bytes 45000000 | tf_op jit(solution)/shard_map/pallas_call | solution.py:87
  118.1 1.9 fusion.52
  123.9 1.9 fusion.37
  126.7 2.2 convolution_convert_fusion.1
  131.6 1.8 fusion.43
  133.4 1.8 fusion.45
  135.2 5.2 %fusion.4.lin_ref = bf16[96,48,128]{2,1,0:T(8,128)(2,1)S(1)} fusion(f32[96,48,128]{2,0,1:T(8,128)S(1)} %fusion.41, f32[96,48,128]{2,0,1:T(8,128)S(1)} %fusion.43, f32[96,48,128]{2,0,1:T(8,128)S(1)} %fusion.45, f32[48,128,96]{1,2,0:T(8,128)S(1)} %fusion.27), kind=kLoop, calls=%fused_computation.8 | loop fusion | flops 2359296 | bytes 10616832 | tf_op jit(solution)/shard_map/convert_element_type | solution.py:429
  140.4 22.3 %shard_map.154 = (bf16[128,1024]{1,0:T(8,128)(2,1)S(1)}, f32[8,1024]{1,0:T(8,128)S(1)}, bf16[12,192,128]{2,1,0:T(8,128)(2,1)S(1)}) custom-call(bf16[128,1024]{1,0:T(8,128)(2,1)S(1)} %convolution_convert_fusion.3.part_ref, f32[32,1024]{1,0:T(8,128)S(1)} %get-tuple-element.20.pre_ref, bf16[96,48,128]{2,1,0:T(8,128)(2,1)S(1)} %fusion.4.lin_ref), custom_call_target="tpu_custom_call" | custom-call | bytes 105000000 | tf_op jit(solution)/shard_map/pallas_call | solution.py:87
  164.1 2.7 convolution_convert_fusion
  172.9 4.9 %fusion.53 = bf16[128,16,192]{2,1,0:T(8,128)(2,1)} fusion(bf16[128,96,16]{1,2,0:T(8,128)(2,1)} %copy.59, bf16[128,96,192]{2,1,0:T(8,128)(2,1)} %copy.43), kind=kOutput, calls=%fused_computation.96 | convolution fusion | flops 75497472 | bytes 5898240 | tf_op jit(solution)/shard_map/bfk,bfe->keb/dot_general | solution.py:465
  177.8 2.6 copy.61
  180.5 2.7 fusion.40
  184.4 77.1 %shard_map.155 = (bf16[112,48,128]{2,1,0:T(8,128)(2,1)S(1)}, f32[32,1152]{1,0:T(8,128)S(1)}, f32[32,1536]{1,0:T(8,128)S(1)}) custom-call(bf16[16,2,32,1152]{3,2,1,0:T(8,128)(2,1)S(1)} %bitcast.125, bf16[16,2,32,1536]{3,2,1,0:T(8,128)(2,1)} %bitcast.133, bf16[12,192,128]{2,1,0:T(8,128)(2,1)S(1)} %get-tuple-element.54.glc_ref, bf16[16,192,128]{2,1,0:T(8,128)(2,1)S(1)} %bitcast.126), custom_call_target="tpu_custom_call" | custom-call | bytes 180000000 | tf_op jit(solution)/shard_map/pallas_call | solution.py:87
  262.2 1.8 convolution_bitcast_fusion.2
  264.0 1.9 convolution_bitcast_fusion.1
  265.9 1.8 convolution_bitcast_fusion
  267.7 26.1 %shard_map.156 = f32[112,128]{1,0:T(8,128)S(1)} custom-call(f32[4,96,128]{2,1,0:T(8,128)S(1)} %select_maximum_fusion.part_ref, f32[16,128]{1,0:T(8,128)S(1)} %select_maximum_fusion.3.rows_ref), custom_call_target="tpu_custom_call" | custom-call | bytes 60000000 | tf_op jit(solution)/shard_map/pallas_call | solution.py:87
  (96 shorter events, 30.1 us)
Async XLA Ops:
  0.6 101.1 %copy-start = (bf16[1024,1536]{1,0:T(8,128)(2,1)S(1)}, bf16[1024,1536]{1,0:T(8,128)(2,1)}, u32[]{:S(2)}) copy-start(bf16[1024,1536]{1,0:T(8,128)(2,1)} %param.11) | copy-start | bytes 9437188
  6.4 123.0 %collective-permute-start.2 = (bf16[96,48,128]{2,0,1:T(8,128)(2,1)}, bf16[96,48,128]{2,0,1:T(8,128)(2,1)}, u32[]{:S(2)}, u32[]{:S(2)}) collective-permute-start(bf16[96,48,128]{2,0,1:T(8,128)(2,1)} %bitcast.121), channel_id=1, source_target_pairs={{0,3},{1,0},{2,1},{3,2},{4,7},{5,4},{6,5},{7,6},{8,11},{9,8},{10,9... | collective-permute-start | bytes 3538952 | tf_op jit(solution)/shard_map/ppermute | solution.py:376
  11.4 120.2 %collective-permute-start.1 = (bf16[96,48,128]{2,0,1:T(8,128)(2,1)}, bf16[96,48,128]{2,0,1:T(8,128)(2,1)}, u32[]{:S(2)}, u32[]{:S(2)}) collective-permute-start(bf16[96,48,128]{2,0,1:T(8,128)(2,1)} %bitcast.122), channel_id=1, source_target_pairs={{0,2},{1,3},{2,0},{3,1},{4,6},{5,7},{6,4},{7,5},{8,10},{9,11},{10,... | collective-permute-start | bytes 3538952 | tf_op jit(solution)/shard_map/ppermute | solution.py:376
  13.1 9.7 %copy-start.24 = (bf16[96,16]{0,1:T(8,128)(2,1)S(1)}, bf16[96,16]{0,1:T(8,128)(2,1)}, u32[]{:S(2)}) copy-start(bf16[96,16]{0,1:T(8,128)(2,1)} %param.10) | copy-start | bytes 9220
  13.1 120.3 %collective-permute-start = (bf16[96,48,128]{2,0,1:T(8,128)(2,1)}, bf16[96,48,128]{2,0,1:T(8,128)(2,1)}, u32[]{:S(2)}, u32[]{:S(2)}) collective-permute-start(bf16[96,48,128]{2,0,1:T(8,128)(2,1)} %bitcast.123), channel_id=1, source_target_pairs={{0,1},{1,2},{2,3},{3,0},{4,5},{5,6},{6,7},{7,4},{8,9},{9,10},{10,1... | collective-permute-start | bytes 3538952 | tf_op jit(solution)/shard_map/ppermute | solution.py:376
  22.8 5.0 %copy-start.16 = (bf16[96,96]{1,0:T(8,128)(2,1)S(1)}, bf16[96,96]{1,0:T(8,128)(2,1)}, u32[]{:S(2)}) copy-start(bf16[96,96]{1,0:T(8,128)(2,1)} %param.14) | copy-start | bytes 55300
  101.7 1.2 copy-start.13
  101.7 1.2 copy-start.7
  101.7 16.3 %copy-start.9 = (bf16[1024,1152]{1,0:T(8,128)(2,1)S(1)}, bf16[1024,1152]{1,0:T(8,128)(2,1)}, u32[]{:S(2)}) copy-start(bf16[1024,1152]{1,0:T(8,128)(2,1)} %param.13) | copy-start | bytes 7077892
  119.9 2.4 copy-start.20
  121.0 2.8 copy-start.8
  122.3 3.5 %copy-start.10 = (bf16[1024,1152]{1,0:T(8,128)(2,1)S(1)}, bf16[1024,1152]{1,0:T(8,128)(2,1)}, u32[]{:S(2)}) copy-start(bf16[1024,1152]{1,0:T(8,128)(2,1)} %param.13) | copy-start | bytes 7077892
  126.7 2.2 copy-start.11
  126.7 2.2 copy-start.17
  162.7 4.4 %copy-start.2 = (bf16[12,192,128]{2,1,0:T(8,128)(2,1)}, bf16[12,192,128]{2,1,0:T(8,128)(2,1)S(1)}, u32[]{:S(2)}) copy-start(bf16[12,192,128]{2,1,0:T(8,128)(2,1)S(1)} %get-tuple-element.22) | copy-start | bytes 1769476
  162.8 1.4 copy-start.14
  166.8 1.1 copy-start.15
  166.8 1.1 copy-start.21
  177.8 2.7 copy-start.19
  177.8 2.7 copy-start.18
  177.8 2.7 copy-start.22
  180.5 2.7 copy-start.1
  183.3 1.1 copy-start.3
  184.4 77.1 %copy-start.12 = (bf16[128,96,48]{0,2,1:T(8,128)(2,1)S(1)}, bf16[128,96,48]{0,2,1:T(8,128)(2,1)}, u32[]{:S(2)}) copy-start(bf16[128,96,48]{0,2,1:T(8,128)(2,1)} %get-tuple-element.50) | copy-start | bytes 3538948
  (5 other events, 3.8 us)

commit v2 on v0

v2 whole, which is shorter than its diff:
```python
import functools

import jax
import jax.numpy as jnp
from jax import lax
from jax.experimental import pallas as pl
from jax.experimental.pallas import tpu as pltpu
from jax.sharding import PartitionSpec as P

MESH = pl.DeviceIdType.MESH
VMEM = pltpu.VMEM
F32 = jnp.float32
BF16 = jnp.bfloat16
LIMIT = 24 * 1024 * 1024


class Place:
    def __init__(self):
        batch, field = lax.axis_index("batch"), lax.axis_index("field")
        self.batch, self.field = batch, field
        self.y, self.zh = lax.rem(field, 4), lax.div(field, 4)
        self.core = lax.rem(batch, 2)
        self.zl = lax.rem(lax.div(batch, 2), 4)
        self.x = lax.div(batch, 8)

    def to_y(self, k):
        other = lax.rem(self.y + k, 4)
        return other, (self.batch, self.zh * 4 + other)

    def to_zh(self):
        other = 1 - self.zh
        return other, (self.batch, other * 4 + self.y)

    def to_core(self):
        other = 1 - self.core
        return other, (self.x * 8 + self.zl * 2 + other, self.field)

    def to_x(self, k):
        other = lax.rem(self.x + k, 4)
        return other, (other * 8 + self.zl * 2 + self.core, self.field)

    def to_zl(self, k):
        other = lax.rem(self.zl + k, 4)
        return other, (self.x * 8 + other * 2 + self.core, self.field)

    def y_group(self):
        return [self.to_y(k)[1] for k in (1, 2, 3)]

    def field_group(self):
        return self.y_group() + [self.to_zh()[1]]

    def batch_group(self):
        return [self.to_core()[1]] + [self.to_x(k)[1] for k in (1, 2, 3)] + [self.to_zl(k)[1] for k in (1, 2, 3)]


def greet(peers, work=None):
    barrier = pltpu.get_barrier_semaphore()
    for peer in peers:
        pl.semaphore_signal(barrier, inc=1, device_id=peer, device_id_type=MESH)
    if work is not None:
        work()
    pl.semaphore_wait(barrier, len(peers))


def send(src, dst, sems, index, peer):
    copy = pltpu.make_async_remote_copy(
        src_ref=src,
        dst_ref=dst,
        send_sem=sems.at[0, index],
        recv_sem=sems.at[1, index],
        device_id=peer,
        device_id_type=MESH,
    )
    copy.start()
    return copy


def params(collective_id):
    return pltpu.CompilerParams(
        collective_id=collective_id, has_side_effects=True, vmem_limit_bytes=LIMIT
    )


def cost(us):
    return pl.CostEstimate(flops=0, bytes_accessed=int(us * 3.0e6), transcendentals=0)


def call(kernel, outs, scratch, collective_id, us, *args):
    return pl.pallas_call(
        kernel,
        out_shape=[jax.ShapeDtypeStruct(shape, dtype) for shape, dtype in outs],
        in_specs=[pl.BlockSpec(memory_space=VMEM)] * len(args),
        out_specs=[pl.BlockSpec(memory_space=VMEM)] * len(outs),
        scratch_shapes=scratch,
        compiler_params=params(collective_id),
        cost_estimate=cost(us),
    )(*args)


def rows(start, size):
    return pl.ds(pl.multiple_of(start * size, size), size)


def field_sum(at, part_ref, got, mine, other, sems, between):
    step = part_ref.shape[0] // 4
    copies = []
    for k in (1, 2, 3):
        y, peer = at.to_y(k)
        copies.append(send(part_ref.at[rows(y, step)], got.at[k - 1], sems, k - 1, peer))
    for copy in copies:
        copy.wait()
    mine[...] = (
        part_ref[rows(at.y, step)].astype(F32)
        + got[0].astype(F32)
        + got[1].astype(F32)
        + got[2].astype(F32)
    ).astype(BF16)
    copy = send(mine, other, sems, 3, at.to_zh()[1])
    between()
    copy.wait()
    return mine[...].astype(F32) + other[...].astype(F32)


def gather_rows(at, out_ref, sems):
    own = rows(at.y, out_ref.shape[0] // 4)
    return [send(out_ref.at[own], out_ref.at[own], sems, 3 + k, at.to_y(k)[1]) for k in (1, 2, 3)]


def mean0(values):
    return jnp.sum(values, axis=0, keepdims=True) * (1.0 / values.shape[0])


def norm(raw, cot, gain):
    centre = raw - mean0(raw)
    rstd = lax.rsqrt(mean0(centre * centre) + 1e-05)
    normed = centre * rstd
    dn = cot * gain
    grad = rstd * (dn - mean0(dn) - normed * mean0(dn * normed))
    return normed * gain, cot * normed, grad


def front_kernel(
    pieces,
    part_ref,
    wl_ref,
    emb_ref,
    up_ref,
    bias_ref,
    wl_out,
    emb_out,
    flat_ref,
    hidden_ref,
    pre_ref,
    cgot,
    cmine,
    cother,
    comp,
    compf,
    embf,
    part,
    got,
    mine,
    other,
    csems,
    wsems,
    esems,
    psems,
):
    at = Place()
    fields, width, examples = emb_ref.shape
    step, kk = width // 4, part_ref.shape[1]
    scale = float(width) ** (-0.5)
    block = embf.shape[0]
    size = fields // pieces
    background = []

    def piece(p):
        here = pl.ds(p * size, size)
        for k in (1, 2, 3):
            y, peer = at.to_y(k)
            background.append(
                send(emb_ref.at[here, rows(y, step), :], emb_out.at[k, here], esems, p * 3 + k - 1, peer)
            )

    def own_part():
        wl_out[0] = jnp.zeros(wl_out.shape[1:], BF16)
        wl_out[0, :, : wl_ref.shape[1]] = wl_ref[...]
        emb_out[0] = emb_ref[:, rows(at.y, step), :]

    greet(at.field_group(), own_part)
    copies = []
    for k in (1, 2, 3):
        y, peer = at.to_y(k)
        copies.append(send(part_ref.at[rows(y, step)], cgot.at[k - 1], csems, k - 1, peer))
    for k in (1, 2, 3):
        background.append(send(wl_out.at[0], wl_out.at[k], wsems, k - 1, at.to_y(k)[1]))
    for copy in copies:
        copy.wait()
    cmine[...] = (
        part_ref[rows(at.y, step)].astype(F32)
        + cgot[0].astype(F32)
        + cgot[1].astype(F32)
        + cgot[2].astype(F32)
    ).astype(BF16)
    copy = send(cmine, cother, csems, 3, at.to_zh()[1])
    piece(0)
    piece(1)
    copy.wait()
    own = rows(at.y, step)
    comp[own] = (cmine[...].astype(F32) + cother[...].astype(F32)).astype(BF16)
    copies = [send(comp.at[own], comp.at[own], csems, 3 + k, at.to_y(k)[1]) for k in (1, 2, 3)]
    for copy in copies:
        copy.wait()
    compf[...] = comp[...].astype(F32)

    def interact(start, stop):
        @pl.loop(start, stop)
        def _(i):
            embf[...] = emb_ref[pl.ds(i * block, block)].astype(F32)

            def terms(e, totals):
                c = compf[e]
                return tuple(t + c * embf[j, pl.ds(e, 1), :] for j, t in enumerate(totals))

            totals = lax.fori_loop(
                0, width, terms, tuple(jnp.zeros((kk, examples), F32) for _ in range(block)), unroll=8
            )
            for j in range(block):
                flat_ref[i * block + j] = (totals[j] * scale).astype(BF16)

    blocks = fields // block
    cuts = [blocks * p // 3 for p in range(4)]
    for p in range(3):
        piece(2 + p)
        interact(cuts[p], cuts[p + 1])

    flat = flat_ref[...].reshape(fields * kk, examples)
    units = up_ref.shape[0]
    quarter = units // 4

    @pl.loop(0, 4)
    def _(r):
        part[rows(r, quarter)] = jnp.dot(
            up_ref[rows(r, quarter), :], flat, preferred_element_type=F32
        ).astype(BF16)

    def after(p):
        def go():
            if p < pieces:
                piece(p)

        return go

    bias = jnp.transpose(jnp.broadcast_to(bias_ref[:, rows(at.y, quarter)], (examples, quarter)))
    pre = field_sum(at, part, got, mine, other, psems, after(5)) + bias
    pre_ref[...] = pre
    hidden_ref[rows(at.y, quarter)] = (pre / (1.0 + jnp.exp(-pre))).astype(BF16)
    for copy in gather_rows(at, hidden_ref, psems):
        copy.wait()
    for copy in background:
        copy.wait()


class BatchSum:
    def __init__(self, at, ref, one, two, three, sems, out):
        self.at, self.ref, self.one, self.two, self.three, self.sems, self.out = (
            at, ref, one, two, three, sems, out,
        )

    def first(self):
        core, peer = self.at.to_core()
        self.copies = [send(self.ref.at[:, core], self.one, self.sems, 0, peer)]

    def wait(self):
        for copy in self.copies:
            copy.wait()

    def second(self):
        self.wait()
        one = self.one

        @pl.loop(0, 16)
        def _(j):
            one[j] = (one[j].astype(F32) + self.ref[j, self.at.core].astype(F32)).astype(BF16)

        self.copies = []
        for k in (1, 2, 3):
            x, peer = self.at.to_x(k)
            self.copies.append(send(one.at[pl.ds(x * 4, 4)], self.two.at[k - 1], self.sems, k, peer))

    def third(self):
        self.wait()
        for j in range(4):
            total = self.one[self.at.x * 4 + j].astype(F32)
            for k in range(3):
                total = total + self.two[k, j].astype(F32)
            self.two[0, j] = total.astype(BF16)
        self.copies = []
        for k in (1, 2, 3):
            z, peer = self.at.to_zl(k)
            self.copies.append(send(self.two.at[0, z], self.three.at[k - 1], self.sems, 3 + k, peer))

    def last(self):
        self.wait()
        total = self.two[0, self.at.zl].astype(F32)
        for k in range(3):
            total = total + self.three[k].astype(F32)
        self.out[...] = total


def middle_kernel(
    hidden_ref,
    pre_ref,
    down_ref,
    cot_ref,
    gain_ref,
    lin_ref,
    fm_ref,
    gain_out,
    gpre_ref,
    bias_out,
    raw_ref,
    down_out,
    gfm_ref,
    part,
    got,
    mine,
    other,
    lmine,
    lother,
    dpart,
    d1,
    d2,
    d3,
    hsems,
    lsems,
    dsems,
):
    at = Place()
    units, examples = hidden_ref.shape
    width, quarter = gain_ref.shape[0], units // 4
    chunk, step = raw_ref.shape[0], raw_ref.shape[1] // 4
    half = 4 * chunk
    zh, zpeer = at.to_zh()
    lcopies = []

    def linear(j):
        field = lax.rem(at.y + 1 + j, 4) * chunk
        lcopies.append(
            send(lin_ref.at[pl.ds(zh * half + field, chunk)], lother.at[pl.ds(field, chunk)], lsems, j, zpeer)
        )

    gain = gain_ref[...]

    def forward():
        hidden = jnp.transpose(hidden_ref[...].astype(F32)).astype(BF16)
        gain_total = jnp.zeros((width, examples), F32)
        for n in range(0, cot_ref.shape[0], 2):
            raw = jnp.transpose(
                jnp.dot(hidden, down_ref[:, n * width : (n + 2) * width], preferred_element_type=F32)
            )
            for m in range(2):
                out, term, grad = norm(
                    raw[m * width : (m + 1) * width], cot_ref[n + m].astype(F32), gain
                )
                fm_ref[n + m] = out.astype(BF16)
                gain_total = gain_total + term
                gfm_ref[n + m] = grad.astype(BF16)
        gain_out[...] = gain_total

    greet(at.field_group() + at.batch_group(), forward)
    linear(0)
    linear(1)
    gfm = gfm_ref[...].reshape(down_ref.shape[1], examples)

    @pl.loop(0, 4)
    def _(r):
        part[rows(r, quarter)] = jnp.dot(
            down_ref[rows(r, quarter), :], gfm, preferred_element_type=F32
        ).astype(BF16)

    copies = []
    for k in (1, 2, 3):
        y, peer = at.to_y(k)
        copies.append(send(part.at[rows(y, quarter)], got.at[k - 1], hsems, k - 1, peer))

    @pl.loop(0, 4)
    def _(r):
        block = lax.dot_general(
            hidden_ref[rows(r, quarter), :],
            gfm,
            (((1,), (1,)), ((), ())),
            preferred_element_type=F32,
        ).astype(BF16)
        dpart[rows(r, 4)] = block.reshape((4,) + dpart.shape[1:])

    down = BatchSum(at, dpart, d1, d2, d3, dsems, down_out)
    down.first()
    for copy in copies:
        copy.wait()
    mine[...] = (
        part[rows(at.y, quarter)].astype(F32)
        + got[0].astype(F32)
        + got[1].astype(F32)
        + got[2].astype(F32)
    ).astype(BF16)
    copy = send(mine, other, hsems, 3, zpeer)
    linear(2)
    linear(3)
    down.second()
    pre = pre_ref[...]
    sigma = 1.0 / (1.0 + jnp.exp(-pre))
    slope = sigma * (1.0 + pre * (1.0 - sigma))
    copy.wait()
    grad = (mine[...].astype(F32) + other[...].astype(F32)) * slope
    gpre_ref[rows(at.y, quarter)] = grad.astype(BF16)
    copies = gather_rows(at, gpre_ref, hsems)
    bias_out[...] = jnp.sum(grad, axis=1, keepdims=True)
    zbase = at.zh * half
    own = rows(at.y, step)
    for j in range(4):
        lcopies[j].wait()
        field, peer = at.to_y(j + 1)
        for n in range(chunk):
            lmine[field * chunk + n] = (
                lin_ref[zbase + field * chunk + n].astype(F32) + lother[field * chunk + n].astype(F32)
            ).astype(BF16)
        if j < 3:
            copies.append(
                send(lmine.at[pl.ds(field * chunk, chunk)], raw_ref.at[:, own, :], lsems, 4 + j, peer)
            )
        if j == 1:
            down.third()
    raw_ref[:, own, :] = lmine[pl.ds(at.y * chunk, chunk)]
    down.last()
    for copy in copies:
        copy.wait()


def grads_kernel(
    raw,
    up_ref,
    inter_ref,
    emb_ref,
    cot_ref,
    gain_ref,
    rows_ref,
    out_ref,
    gather_ref,
    gcomp_ref,
    up_out,
    rows_out,
    interf,
    embf,
    cb,
    cgot,
    cmine,
    cother,
    glc,
    u1,
    u2,
    u3,
    rgot,
    rmine,
    rsum,
    rother,
    ysems,
    zsems,
    csems,
    usems,
    rsems,
):
    at = Place()
    fields, width, examples = emb_ref.shape
    kk, step = inter_ref.shape[1], width // 4
    scale = float(width) ** (-0.5)
    out_fields = cot_ref.shape[0]
    half = 4 * out_fields
    zh, zpeer = at.to_zh()
    zbase = at.zh * half
    own_part = rows(at.y, step)
    gain = gain_ref[...]

    def linear():
        rsum[...] = jnp.zeros_like(rsum)

        @pl.loop(0, out_fields)
        def _(n):
            out, term, grad = norm(raw[n].astype(F32), cot_ref[n].astype(F32), gain)
            out_ref[n] = out.astype(BF16)
            rsum[...] += term
            glc[n] = grad.astype(BF16)

    greet(at.field_group() + at.batch_group(), linear)
    own = pl.ds(zbase + at.y * out_fields, out_fields)
    gcopies = []
    for k in (1, 2, 3):
        y, peer = at.to_y(k)
        gcopies.append(send(glc.at[:, rows(y, step), :], gather_ref.at[own], ysems, k - 1, peer))
    gather_ref[own] = glc[:, own_part, :]
    zcopies = [send(gather_ref.at[own], gather_ref.at[own], zsems, 0, zpeer)]
    n_bias = rows_ref.shape[0] - 4
    rmine[...] = rows_ref[...]
    rmine[n_bias : n_bias + 1, :width] = rmine[n_bias : n_bias + 1, :width] + jnp.sum(
        jnp.transpose(rsum[...]), axis=0, keepdims=True
    )
    rcopies = [send(rmine, rgot.at[k - 1], rsems, k - 1, at.to_y(k)[1]) for k in (1, 2, 3)]
    up = BatchSum(at, up_ref, u1, u2, u3, usems, up_out)
    up.first()
    interf[...] = inter_ref[...].astype(F32)
    block = embf.shape[1]

    def compression(start, stop):
        @pl.loop(start, stop)
        def _(i):
            embf[...] = emb_ref[:, rows(i, block), :].astype(F32)

            def terms(f, totals):
                g = interf[f]
                return tuple(t + g * embf[f, pl.ds(j, 1), :] for j, t in enumerate(totals))

            totals = lax.fori_loop(
                0, fields, terms, tuple(jnp.zeros((kk, examples), F32) for _ in range(block)), unroll=4
            )
            for j in range(block):
                cb[i * block + j] = totals[j].astype(BF16)

    blocks = width // block
    compression(0, blocks // 3)
    up.second()
    for k in (1, 2, 3):
        gcopies[k - 1].wait()
        source = lax.rem(at.y + 4 - k, 4)
        there = pl.ds(zbase + source * out_fields, out_fields)
        zcopies.append(send(gather_ref.at[there], gather_ref.at[there], zsems, k, zpeer))
    for copy in rcopies:
        copy.wait()
    rmine[...] = (rmine[...] + rgot[1]) + (rgot[0] + rgot[2])
    rcopy = send(rmine, rother, rsems, 3, zpeer)
    compression(blocks // 3, blocks)
    ccopies = []
    for k in (1, 2, 3):
        y, peer = at.to_y(k)
        ccopies.append(send(cb.at[rows(y, step)], cgot.at[k - 1], csems, k - 1, peer))
    for copy in ccopies:
        copy.wait()
    cmine[...] = (
        cb[own_part].astype(F32)
        + cgot[0].astype(F32)
        + cgot[1].astype(F32)
        + cgot[2].astype(F32)
    ).astype(BF16)
    ccopy = send(cmine, cother, csems, 3, zpeer)
    up.third()
    rcopy.wait()
    rows_out[...] = rmine[...] + rother[...]
    ccopy.wait()
    gcomp_ref[...] = ((cmine[...].astype(F32) + cother[...].astype(F32)) * scale).astype(BF16)
    up.last()
    for copy in zcopies:
        copy.wait()


def small_kernel(
    nl, part_ref, rows_ref, lin_ref, comp_ref, rows_out, psend, ygot, one, xmine, xgot, zmine, zgot, sems
):
    at = Place()
    fields, kk = lin_ref.shape[0], comp_ref.shape[0]
    psend[...] = part_ref[...].astype(BF16)
    greet(at.y_group() + at.batch_group())
    copies = []
    for k in (1, 2, 3):
        copies.append(send(psend.at[k], ygot.at[k - 1], sems, k - 1, at.to_y(4 - k)[1]))
    half = rows_ref.shape[0]
    one[0, fields : fields + half] = rows_ref[:, :128]
    one[0, fields + half :] = rows_ref[:, 128:]
    for copy in copies:
        copy.wait()
    one[0, :fields] = (
        part_ref[0] + ygot[0].astype(F32) + ygot[1].astype(F32) + ygot[2].astype(F32)
    )
    send(one.at[0], one.at[1], sems, 3, at.to_core()[1]).wait()
    xmine[...] = (one[0] + one[1]).astype(BF16)
    copies = [send(xmine, xgot.at[k - 1], sems, 3 + k, at.to_x(k)[1]) for k in (1, 2, 3)]
    for copy in copies:
        copy.wait()
    zmine[...] = (
        (xmine[...].astype(F32) + xgot[1].astype(F32))
        + (xgot[0].astype(F32) + xgot[2].astype(F32))
    ).astype(BF16)
    copies = [send(zmine, zgot.at[k - 1], sems, 6 + k, at.to_zl(k)[1]) for k in (1, 2, 3)]
    for copy in copies:
        copy.wait()
    total = (zmine[...].astype(F32) + zgot[1].astype(F32)) + (
        zgot[0].astype(F32) + zgot[2].astype(F32)
    )
    lin_ref[...] = total[:fields, :nl]
    comp_ref[...] = jnp.transpose(total[:fields])[nl : nl + kk]
    rows_out[:, :128] = total[fields : fields + half]
    rows_out[:, 128:] = total[fields + half :]


def local(embeddings, compress, w_up, up_bias, w_down, w_linear, ln_gain, cot_fm, cot_lc):
    examples, fields, width = embeddings.shape
    units, kk, nl = w_up.shape[0], compress.shape[1], w_linear.shape[1]
    part, quarter, own_rows = width // 4, units // 4, units // 32
    turned = embeddings.transpose(1, 2, 0)
    gain = jnp.broadcast_to(ln_gain.reshape(-1, 1), (width, examples))
    comp_part = jnp.einsum("feb,fk->ekb", turned, compress, preferred_element_type=F32).astype(BF16)
    cot_first, cot_second = cot_fm.transpose(1, 2, 0), cot_lc.transpose(1, 2, 0)
    pieces, block = 6, 8

    def stages(columns):
        return [
            VMEM((16, own_rows, columns), BF16),
            VMEM((3, 4, own_rows, columns), BF16),
            VMEM((3, own_rows, columns), BF16),
        ]

    row_scratch = [
        VMEM((units, examples), BF16),
        VMEM((3, quarter, examples), BF16),
        VMEM((quarter, examples), BF16),
        VMEM((quarter, examples), BF16),
    ]
    wl_all, spread, flat, hidden, hidden_pre = call(
        functools.partial(front_kernel, pieces),
        [
            ((4, fields, 128), BF16),
            ((4, fields, part, examples), BF16),
            ((fields, kk, examples), BF16),
            ((units, examples), BF16),
            ((quarter, examples), F32),
        ],
        [
            VMEM((3, part, kk, examples), BF16),
            VMEM((part, kk, examples), BF16),
            VMEM((part, kk, examples), BF16),
            VMEM((width, kk, examples), BF16),
            VMEM((width, kk, examples), F32),
            VMEM((block, width, examples), F32),
        ]
        + row_scratch
        + [
            pltpu.SemaphoreType.DMA((2, 7)),
            pltpu.SemaphoreType.DMA((2, 3)),
            pltpu.SemaphoreType.DMA((2, 3 * pieces)),
            pltpu.SemaphoreType.DMA((2, 7)),
        ],
        0,
        80,
        comp_part,
        w_linear,
        turned,
        w_up,
        up_bias.reshape(1, -1),
    )
    spread = spread.reshape(4 * fields, part, examples)
    lin = jnp.einsum(
        "feb,fn->neb", spread, wl_all.reshape(4 * fields, 128)[:, :nl], preferred_element_type=F32
    ).astype(BF16)
    columns = cot_first.shape[0] * width
    fm_out, gain_fm, grad_pre, bias_part, lc_raw, grad_down = call(
        middle_kernel,
        [
            (cot_first.shape, BF16),
            ((width, examples), F32),
            ((units, examples), BF16),
            ((quarter, 1), F32),
            (cot_second.shape, BF16),
            ((own_rows, columns), F32),
        ],
        [VMEM(cot_first.shape, BF16)]
        + row_scratch
        + [
            VMEM((nl // 2, part, examples), BF16),
            VMEM((nl // 2, part, examples), BF16),
            VMEM((16, 2, own_rows, columns), BF16),
        ]
        + stages(columns)
        + [
            pltpu.SemaphoreType.DMA((2, 7)),
            pltpu.SemaphoreType.DMA((2, 7)),
            pltpu.SemaphoreType.DMA((2, 7)),
        ],
        1,
        35,
        hidden,
        hidden_pre,
        w_down,
        cot_first,
        gain,
        lin,
    )
    flat = flat.reshape(fields * kk, examples)
    up_part = jnp.einsum("hb,jb->hj", grad_pre, flat, preferred_element_type=F32).astype(BF16)
    grad_inter = (
        jnp.einsum("hj,hb->jb", w_up, grad_pre, preferred_element_type=F32)
        .astype(BF16)
        .reshape(fields, kk, examples)
    )
    n_bias = units // 256
    y = lax.rem(lax.axis_index("field"), 4)
    bias_rows = lax.dynamic_update_slice_in_dim(
        jnp.zeros((units,), F32), 0.5 * bias_part.reshape(-1), y * quarter, axis=0
    ).reshape(n_bias, 256)
    gain_row = jnp.pad(jnp.sum(gain_fm, axis=1), (0, 256 - width)).reshape(1, 256)
    extra = jnp.pad(jnp.concatenate([bias_rows, gain_row]), ((0, 3), (0, 0)))

    out_fields, n_extra, slab = nl // 8, extra.shape[0], 16
    lc_out, gathered, grad_comp, grad_up, extra = call(
        grads_kernel,
        [
            (cot_second.shape, BF16),
            ((nl, part, examples), BF16),
            ((part, kk, examples), BF16),
            ((own_rows, fields * kk), F32),
            (extra.shape, F32),
        ],
        [
            VMEM((fields, kk, examples), F32),
            VMEM((fields, slab, examples), F32),
            VMEM((width, kk, examples), BF16),
            VMEM((3, part, kk, examples), BF16),
            VMEM((part, kk, examples), BF16),
            VMEM((part, kk, examples), BF16),
            VMEM(cot_second.shape, BF16),
        ]
        + stages(fields * kk)
        + [
            VMEM((3,) + extra.shape, F32),
            VMEM(extra.shape, F32),
            VMEM((width, examples), F32),
            VMEM(extra.shape, F32),
            pltpu.SemaphoreType.DMA((2, 3)),
            pltpu.SemaphoreType.DMA((2, 4)),
            pltpu.SemaphoreType.DMA((2, 4)),
            pltpu.SemaphoreType.DMA((2, 7)),
            pltpu.SemaphoreType.DMA((2, 4)),
        ],
        2,
        45,
        lc_raw,
        up_part.reshape(16, 2, own_rows, fields * kk),
        grad_inter,
        turned,
        cot_second,
        gain,
        extra,
    )
    mixed = jnp.concatenate(
        [
            jnp.einsum("feb,neb->fn", spread, gathered, preferred_element_type=F32),
            jnp.einsum("feb,ekb->fk", spread, grad_comp, preferred_element_type=F32),
            jnp.zeros((4 * fields, 128 - nl - kk), F32),
        ],
        axis=1,
    ).reshape(4, fields, 128)
    total_rows = fields + 2 * n_extra
    grad_linear, grad_compress, extra = call(
        functools.partial(small_kernel, nl),
        [((fields, nl), F32), ((kk, fields), F32), (extra.shape, F32)],
        [
            VMEM((4, fields, 128), BF16),
            VMEM((3, fields, 128), BF16),
            VMEM((2, total_rows, 128), F32),
            VMEM((total_rows, 128), BF16),
            VMEM((3, total_rows, 128), BF16),
            VMEM((total_rows, 128), BF16),
            VMEM((3, total_rows, 128), BF16),
            pltpu.SemaphoreType.DMA((2, 10)),
        ],
        3,
        15,
        mixed,
        extra,
    )
    grad_bias = extra[:n_bias].reshape(-1)
    grad_gain = extra[n_bias, :width]
    return (
        fm_out.transpose(2, 0, 1),
        lc_out.transpose(2, 0, 1),
        grad_compress.T,
        grad_up,
        grad_bias,
        grad_down,
        grad_linear,
        grad_gain,
    )


def solution(mesh):
    placed = (
        P("batch", "field", None),
        P("field", None),
        P(None, "field"),
        P(),
        P(None, "field"),
        P("field", None),
        P(),
        P("batch", "field", None),
        P("batch", "field", None),
    )
    return jax.shard_map(
        local,
        mesh=mesh,
        in_specs=placed,
        out_specs=(
            P("batch", "field", None),
            P("batch", "field", None),
            P("field", None),
            P("batch", "field"),
            P(),
            P("batch", "field"),
            P("field", None),
            P(),
        ),
        check_vma=False,
    )
```

time: 1130 us -> 234 us (0.21)
  waiting for transfers between devices: 653 us -> 0 us
  blocking collectives: 367 us -> 0 us
  Pallas kernels: 0 us -> 194 us
  matrix products: 49.9 us -> 16.7 us
  between operations: 14.4 us -> 0.95 us
  other arithmetic: 14 us -> 1.21 us
    psum x3 -> x0, blocking collectives: 367 us -> none  [the longest x1 129 us: local(): lax.psum((comp_local, linear_local, bias_local), 'batch')]
    reduce_scatter x3 -> x0, waiting for transfers between devices: 354 us -> none  [the longest x1 196 us: local(): lax.psum_scatter(linear_partial, 'field', scatter_dimension=1, tiled=True)]
    psum x3 -> x0, waiting for transfers between devices: 300 us -> none  [the longest x1 106 us: local(): hidden_pre = lax.psum(pre_partial, 'field') + up_bias]
    pallas_call x0 -> x4, Pallas kernels: none -> 194 us  [call(): pl.pallas_call(kernel, out_shape=[jax.ShapeDtypeStruct(shape, dtype) for...]
    dot_general x12 -> x6, matrix products: 49.9 us -> 16.7 us  [the longest x1 5.32 us: local(): jnp.einsum('feb,fk->ekb', turned, compress, preferred_element_type=F32)]
  transfers between devices with their start and end apart: 7 -> 0, of which waited for: 6 -> 0; matrix products, arithmetic and copies ran while one was open for 5% -> 0% of each run, Pallas kernels for 0% -> 0%
where the time goes in v2:
time: 234 us
  Pallas kernels  194 us (83%)
  local copies, waits for them, and re-layouts  21 us (9%)
  matrix products  16.7 us (7%)
    pallas_call x4, Pallas kernels, call(): pl.pallas_call(kernel, out_shape=[jax.ShapeDtypeStruct(shape, dtype) for...  194 us
    unnamed x54, local copies, waits for them, and re-layouts  18.2 us
    dot_general x1, matrix products, local(): jnp.einsum('feb,fk->ekb', turned, compress, preferred_element_type=F32)  5.32 us

profile of v2, /device:TPU:1, one launch (start us, length us, event | category | flops | bytes accessed | tf_op | source)
XLA Modules:
  0.0 233.9 jit_solution(17923181580356147979)
XLA Ops:
  1.3 5.3 %fusion.12.part_ref = bf16[192,16,128]{2,1,0:T(8,128)(2,1)S(1)} fusion(bf16[96,192,128]{2,1,0:T(8,128)(2,1)} %bitcast.38, bf16[96,16]{0,1:T(8,128)(2,1)S(1)} %copy-done), kind=kOutput, calls=%fused_computation.13 | convolution fusion | flops 75890688 | bytes 5508096 | tf_op jit(solution)/shard_map/feb,fk->ekb/dot_general | solution.py:609
  6.7 1.9 copy-done.3
  8.6 89.0 %shard_map.152 = (bf16[4,96,128]{2,1,0:T(8,128)(2,1)S(1)}, bf16[4,96,48,128]{3,2,1,0:T(8,128)(2,1)S(1)}, bf16[96,16,128]{2,1,0:T(8,128)(2,1)S(1)}, bf16[1024,128]{1,0:T(8,128)(2,1)S(1)}, f32[256,128]{1,0:T(8,128)S(1)}) custom-call(bf16[192,16,128]{2,1,0:T(8,128)(2,1)S(1)} %fusion.12.part_ref, bf16[96,96]{1,0:T(8,128)(2,1)S(1)} %copy-done.18, ...), custom_call_target="tpu_custom_call" | custom-call | bytes 240000000 | tf_op jit(solution)/shard_map/pallas_call | solution.py:89
  97.6 1.0 fusion.6
  98.6 1.3 copy-done.6
  101.1 39.3 %shard_map.153 = (bf16[6,192,128]{2,1,0:T(8,128)(2,1)S(1)}, f32[192,128]{1,0:T(8,128)S(1)}, bf16[1024,128]{1,0:T(8,128)(2,1)S(1)}, f32[256,1]{1,0:T(8,128)S(1)},...) custom-call(bf16[1024,128]{1,0:T(8,128)(2,1)S(1)} %get-tuple-element.27.hidden_ref, ...), custom_call_target="tpu_custom_call" | custom-call | bytes 105000000 | tf_op jit(solution)/shard_map/pallas_call | solution.py:89
  140.4 0.8 copy-done.9
  141.2 0.7 copy-done.13
  143.4 1.0 reduce_sum.9
  144.4 3.6 %convolution_convert_fusion = bf16[1024,1536]{1,0:T(8,128)(2,1)} fusion(bf16[1024,128]{1,0:T(8,128)(2,1)S(1)} %get-tuple-element.33, bf16[1536,128]{1,0:T(8,128)(2,1)} %bitcast.51), kind=kOutput, calls=%fused_computation.2 | convolution fusion | flops 404226048 | bytes 3801088 | tf_op jit(solution)/shard_map/hb,jb->hj/dot_general | solution.py:696
  148.1 1.4 fusion.8
  149.5 1.2 copy.30
  150.7 2.3 copy-done.2
  153.0 1.9 copy-done.5
  154.9 1.1 copy-done.8
  156.0 1.1 copy-done.10
  157.0 45.6 %shard_map.154 = (bf16[12,192,128]{2,1,0:T(8,128)(2,1)S(1)}, bf16[96,48,128]{2,1,0:T(8,128)(2,1)S(1)}, bf16[48,16,128]{2,1,0:T(8,128)(2,1)S(1)}, f32[32,1536]{1,0:T(8,128)S(1)}, f32[8,256]{1,0:T(8,128)S(1)}) custom-call(bf16[12,192,128]{2,1,0:T(8,128)(2,1)S(1)} %copy-done.10, bf16[16,2,32,1536]{3,2,1,0:T(8,128)(2,1)S(1)} %bitcast.41, ...), custom_call_target="tpu_custom_call" | custom-call | bytes 135000000 | tf_op jit(solution)/shard_map/pallas_call | solution.py:89
  202.6 4.0 %fusion.16 = f32[384,96]{0,1:T(8,128)S(1)} fusion(bf16[96,48,128]{2,1,0:T(8,128)(2,1)S(1)} %get-tuple-element.38, bf16[384,48,128]{2,1,0:T(8,128)(2,1)} %bitcast.43), kind=kOutput, calls=%fused_computation.15 | convolution fusion | flops 452984832 | bytes 6045696 | tf_op jit(solution)/shard_map/feb,neb->fn/dot_general | solution.py:753
  206.7 1.3 fusion.21
  208.3 20.3 %shard_map.155 = (f32[96,96]{1,0:T(8,128)S(1)}, f32[16,96]{1,0:T(8,128)S(1)}, f32[8,256]{1,0:T(8,128)S(1)}) custom-call(f32[4,96,128]{2,1,0:T(8,128)S(1)} %bitcast.48, f32[8,256]{1,0:T(8,128)S(1)} %get-tuple-element.40.rows_ref), custom_call_target="tpu_custom_call" | custom-call | bytes 45000000 | tf_op jit(solution)/shard_map/pallas_call | solution.py:89
  229.8 0.7 copy.66
  230.6 0.8 copy.67
  232.0 0.7 copy.69
  232.7 0.7 copy.70
  (56 shorter events, 6.0 us)
Async XLA Ops:
  0.6 0.7 copy-start
  0.6 6.0 %copy-start.19 = (f32[1024]{0:T(1024)S(1)}, f32[1024]{0:T(1024)}, u32[]{:S(2)}) copy-start(f32[1024]{0:T(1024)} %param.12) | copy-start | bytes 12292
  0.7 6.0 %copy-start.18 = (bf16[96,96]{1,0:T(8,128)(2,1)S(1)}, bf16[96,96]{1,0:T(8,128)(2,1)}, u32[]{:S(2)}) copy-start(bf16[96,96]{1,0:T(8,128)(2,1)} %wl_ref.1) | copy-start | bytes 55300
  0.7 6.0 %copy-start.1 = (bf16[128,96,192]{0,2,1:T(8,128)(2,1)S(1)}, bf16[128,96,192]{0,2,1:T(8,128)(2,1)}, u32[]{:S(2)}) copy-start(bf16[128,96,192]{0,2,1:T(8,128)(2,1)} %param.9) | copy-start | bytes 14155780
  6.7 1.9 copy-start.3
  97.5 2.4 %copy-start.6 = (bf16[4,96,48,128]{3,2,1,0:T(8,128)(2,1)}, bf16[4,96,48,128]{3,2,1,0:T(8,128)(2,1)S(1)}, u32[]{:S(2)}) copy-start(bf16[4,96,48,128]{3,2,1,0:T(8,128)(2,1)S(1)} %get-tuple-element.30) | copy-start | bytes 14155780
  97.5 42.8 %copy-start.11 = (bf16[96,16,128]{2,1,0:T(8,128)(2,1)}, bf16[96,16,128]{2,1,0:T(8,128)(2,1)S(1)}, u32[]{:S(2)}) copy-start(bf16[96,16,128]{2,1,0:T(8,128)(2,1)S(1)} %get-tuple-element.34) | copy-start | bytes 1179652
  97.6 2.9 %copy-start.20 = (f32[192]{0:T(256)S(1)}, f32[192]{0:T(256)}, u32[]{:S(2)}) copy-start(f32[192]{0:T(256)} %param.15) | copy-start | bytes 2308
  97.6 3.5 %copy-start.7 = (bf16[1024,1152]{1,0:T(8,128)(2,1)S(1)}, bf16[1024,1152]{1,0:T(8,128)(2,1)}, u32[]{:S(2)}) copy-start(bf16[1024,1152]{1,0:T(8,128)(2,1)} %down_ref.1) | copy-start | bytes 7077892
  97.6 3.5 %copy-start.12 = (bf16[128,6,192]{0,2,1:T(8,128)(2,1)S(1)}, bf16[128,6,192]{0,2,1:T(8,128)(2,1)}, u32[]{:S(2)}) copy-start(bf16[128,6,192]{0,2,1:T(8,128)(2,1)} %param.16) | copy-start | bytes 884740
  100.4 47.7 %copy-start.4 = (bf16[1024,1536]{1,0:T(8,128)(2,1)S(1)}, bf16[1024,1536]{1,0:T(8,128)(2,1)}, u32[]{:S(2)}) copy-start(bf16[1024,1536]{1,0:T(8,128)(2,1)} %up_ref.1) | copy-start | bytes 9437188
  140.4 0.8 copy-start.9
  141.2 0.7 copy-start.13
  141.9 0.7 copy-start.15
  142.6 0.6 copy-start.17
  150.7 2.3 %copy-start.2 = (bf16[128,96,192]{0,2,1:T(8,128)(2,1)S(1)}, bf16[128,96,192]{0,2,1:T(8,128)(2,1)}, u32[]{:S(2)}) copy-start(bf16[128,96,192]{0,2,1:T(8,128)(2,1)} %param.9) | copy-start | bytes 14155780
  153.0 1.9 copy-start.5
  154.9 1.1 copy-start.8
  156.0 1.1 copy-start.10
  157.0 49.6 %slice-start = ((s8[4718592]{0:T(1024)(128)(4,1)}), s8[524288]{0:T(1024)(128)(4,1)S(1)}, s32[]{:S(2)}) async-start(s8[4718592]{0:T(1024)(128)(4,1)} %bitcast.44), calls=%async_computation | async-start | bytes 1048576
  202.6 4.1 %slice-start.1 = ((s8[4718592]{0:T(1024)(128)(4,1)}), s8[4194304]{0:T(1024)(128)(4,1)S(1)}, s32[]{:S(2)}) async-start(s8[4718592]{0:T(1024)(128)(4,1)} %bitcast.44), calls=%async_computation.1 | async-start | bytes 8388608
  206.7 23.2 %copy-start.14 = (bf16[6,192,128]{2,1,0:T(8,128)(2,1)S(1)}, bf16[6,192,128]{2,1,0:T(8,128)(2,1)}, u32[]{:S(2)}) copy-start(bf16[6,192,128]{2,1,0:T(8,128)(2,1)} %copy-done.13) | copy-start | bytes 884740
  206.7 26.0 %copy-start.16 = (f32[32,1152]{1,0:T(8,128)S(1)}, f32[32,1152]{1,0:T(8,128)}, u32[]{:S(2)}) copy-start(f32[32,1152]{1,0:T(8,128)} %copy-done.15) | copy-start | bytes 442372

commit v3 on v2

--- a/solution.py
+++ b/solution.py
@@ -11,7 +11,7 @@
 VMEM = pltpu.VMEM
 F32 = jnp.float32
 BF16 = jnp.bfloat16
-LIMIT = 24 * 1024 * 1024
+MIB = 1024 * 1024
 
 
 class Place:
@@ -75,9 +75,9 @@
     return copy
 
 
-def params(collective_id):
+def params(collective_id, mib):
     return pltpu.CompilerParams(
-        collective_id=collective_id, has_side_effects=True, vmem_limit_bytes=LIMIT
+        collective_id=collective_id, has_side_effects=True, vmem_limit_bytes=mib * MIB
     )
 
 
@@ -85,14 +85,14 @@
     return pl.CostEstimate(flops=0, bytes_accessed=int(us * 3.0e6), transcendentals=0)
 
 
-def call(kernel, outs, scratch, collective_id, us, *args):
+def call(kernel, outs, scratch, collective_id, us, mib, *args):
     return pl.pallas_call(
         kernel,
         out_shape=[jax.ShapeDtypeStruct(shape, dtype) for shape, dtype in outs],
         in_specs=[pl.BlockSpec(memory_space=VMEM)] * len(args),
         out_specs=[pl.BlockSpec(memory_space=VMEM)] * len(outs),
         scratch_shapes=scratch,
-        compiler_params=params(collective_id),
+        compiler_params=params(collective_id, mib),
         cost_estimate=cost(us),
     )(*args)
 
@@ -308,40 +308,73 @@
         self.out[...] = total
 
 
-def middle_kernel(
+def back_kernel(
     hidden_ref,
     pre_ref,
     down_ref,
     cot_ref,
     gain_ref,
     lin_ref,
+    flat_ref,
+    up_ref,
+    emb_ref,
+    lcot_ref,
     fm_ref,
-    gain_out,
+    out_ref,
+    gather_ref,
+    gcomp_ref,
+    down_out,
+    up_out,
+    rows_out,
+    gfm_ref,
     gpre_ref,
-    bias_out,
-    raw_ref,
-    down_out,
-    gfm_ref,
     part,
     got,
     mine,
     other,
     lmine,
     lother,
+    raw_ref,
+    glc,
     dpart,
+    upart,
     d1,
     d2,
     d3,
+    u1,
+    u2,
+    u3,
+    interf,
+    embf,
+    cb,
+    cgot,
+    cmine,
+    cother,
+    rsum,
+    rmine,
+    rgot,
+    rtotal,
+    rother,
     hsems,
     lsems,
+    ysems,
+    zsems,
+    csems,
     dsems,
+    usems,
+    rsems,
 ):
     at = Place()
     units, examples = hidden_ref.shape
-    width, quarter = gain_ref.shape[0], units // 4
-    chunk, step = raw_ref.shape[0], raw_ref.shape[1] // 4
+    fields, width = emb_ref.shape[:2]
+    quarter, step, kk = units // 4, width // 4, flat_ref.shape[1]
+    scale = float(width) ** (-0.5)
+    chunk = raw_ref.shape[0]
     half = 4 * chunk
     zh, zpeer = at.to_zh()
+    zbase = at.zh * half
+    own = rows(at.y, step)
+    gain = gain_ref[...]
     lcopies = []
 
     def linear(j):
@@ -350,9 +383,13 @@
             send(lin_ref.at[pl.ds(zh * half + field, chunk)], lother.at[pl.ds(field, chunk)], lsems, j, zpeer)
         )
 
-    gain = gain_ref[...]
+    def column_sums(values):
+        return jnp.sum(jnp.transpose(values), axis=0, keepdims=True)
+
+    n_bias = units // rmine.shape[1]
 
     def forward():
+        rmine[...] = jnp.zeros_like(rmine)
         hidden = jnp.transpose(hidden_ref[...].astype(F32)).astype(BF16)
         gain_total = jnp.zeros((width, examples), F32)
         for n in range(0, cot_ref.shape[0], 2):
@@ -366,7 +403,7 @@
                 fm_ref[n + m] = out.astype(BF16)
                 gain_total = gain_total + term
                 gfm_ref[n + m] = grad.astype(BF16)
-        gain_out[...] = gain_total
+        rsum[...] = gain_total
 
     greet(at.field_group() + at.batch_group(), forward)
     linear(0)
@@ -384,16 +421,18 @@
         y, peer = at.to_y(k)
         copies.append(send(part.at[rows(y, quarter)], got.at[k - 1], hsems, k - 1, peer))
 
-    @pl.loop(0, 4)
-    def _(r):
-        block = lax.dot_general(
-            hidden_ref[rows(r, quarter), :],
-            gfm,
-            (((1,), (1,)), ((), ())),
-            preferred_element_type=F32,
-        ).astype(BF16)
-        dpart[rows(r, 4)] = block.reshape((4,) + dpart.shape[1:])
-
+    def weights(left_ref, right, into):
+        @pl.loop(0, 4)
+        def _(r):
+            block = lax.dot_general(
+                left_ref[rows(r, quarter), :],
+                right,
+                (((1,), (1,)), ((), ())),
+                preferred_element_type=F32,
+            ).astype(BF16)
+            into[rows(r, 4)] = block.reshape((4,) + into.shape[1:])
+
+    weights(hidden_ref, gfm, dpart)
     down = BatchSum(at, dpart, d1, d2, d3, dsems, down_out)
     down.first()
     for copy in copies:
@@ -415,10 +454,10 @@
     grad = (mine[...].astype(F32) + other[...].astype(F32)) * slope
     gpre_ref[rows(at.y, quarter)] = grad.astype(BF16)
     copies = gather_rows(at, gpre_ref, hsems)
-    bias_out[...] = jnp.sum(grad, axis=1, keepdims=True)
-    zbase = at.zh * half
-    own = rows(at.y, step)
-    for j in range(4):
+    rmine[pl.ds(at.y, 1), :] = 0.5 * column_sums(grad)
+    ycopies = []
+
+    def linear_sum(j):
         lcopies[j].wait()
         field, peer = at.to_y(j + 1)
         for n in range(chunk):
@@ -426,88 +465,30 @@
                 lin_ref[zbase + field * chunk + n].astype(F32) + lother[field * chunk + n].astype(F32)
             ).astype(BF16)
         if j < 3:
-            copies.append(
+            ycopies.append(
                 send(lmine.at[pl.ds(field * chunk, chunk)], raw_ref.at[:, own, :], lsems, 4 + j, peer)
             )
-        if j == 1:
-            down.third()
-    raw_ref[:, own, :] = lmine[pl.ds(at.y * chunk, chunk)]
-    down.last()
+
+    linear_sum(0)
     for copy in copies:
         copy.wait()
-
-
-def grads_kernel(
-    raw,
-    up_ref,
-    inter_ref,
-    emb_ref,
-    cot_ref,
-    gain_ref,
-    rows_ref,
-    out_ref,
-    gather_ref,
-    gcomp_ref,
-    up_out,
-    rows_out,
-    interf,
-    embf,
-    cb,
-    cgot,
-    cmine,
-    cother,
-    glc,
-    u1,
-    u2,
-    u3,
-    rgot,
-    rmine,
-    rsum,
-    rother,
-    ysems,
-    zsems,
-    csems,
-    usems,
-    rsems,
-):
-    at = Place()
-    fields, width, examples = emb_ref.shape
-    kk, step = inter_ref.shape[1], width // 4
-    scale = float(width) ** (-0.5)
-    out_fields = cot_ref.shape[0]
-    half = 4 * out_fields
-    zh, zpeer = at.to_zh()
-    zbase = at.zh * half
-    own_part = rows(at.y, step)
-    gain = gain_ref[...]
-
-    def linear():
-        rsum[...] = jnp.zeros_like(rsum)
-
-        @pl.loop(0, out_fields)
-        def _(n):
-            out, term, grad = norm(raw[n].astype(F32), cot_ref[n].astype(F32), gain)
-            out_ref[n] = out.astype(BF16)
-            rsum[...] += term
-            glc[n] = grad.astype(BF16)
-
-    greet(at.field_group() + at.batch_group(), linear)
-    own = pl.ds(zbase + at.y * out_fields, out_fields)
-    gcopies = []
-    for k in (1, 2, 3):
-        y, peer = at.to_y(k)
-        gcopies.append(send(glc.at[:, rows(y, step), :], gather_ref.at[own], ysems, k - 1, peer))
-    gather_ref[own] = glc[:, own_part, :]
-    zcopies = [send(gather_ref.at[own], gather_ref.at[own], zsems, 0, zpeer)]
-    n_bias = rows_ref.shape[0] - 4
-    rmine[...] = rows_ref[...]
-    rmine[n_bias : n_bias + 1, :width] = rmine[n_bias : n_bias + 1, :width] + jnp.sum(
-        jnp.transpose(rsum[...]), axis=0, keepdims=True
-    )
-    rcopies = [send(rmine, rgot.at[k - 1], rsems, k - 1, at.to_y(k)[1]) for k in (1, 2, 3)]
-    up = BatchSum(at, up_ref, u1, u2, u3, usems, up_out)
+    flat = flat_ref[...].reshape(fields * kk, examples)
+    gpre = gpre_ref[...]
+    weights(gpre_ref, flat, upart)
+    up = BatchSum(at, upart, u1, u2, u3, usems, up_out)
     up.first()
-    interf[...] = inter_ref[...].astype(F32)
+    linear_sum(1)
+
+    @pl.loop(0, 6)
+    def _(r):
+        size = fields * kk // 6
+        block = lax.dot_general(
+            up_ref[:, rows(r, size)], gpre, (((0,), (0,)), ((), ())), preferred_element_type=F32
+        ).astype(BF16)
+        interf[rows(r, fields // 6)] = block.astype(F32).reshape(fields // 6, kk, examples)
+
+    linear_sum(2)
+    down.third()
     block = embf.shape[1]
 
     def compression(start, stop):
@@ -526,34 +507,54 @@
                 cb[i * block + j] = totals[j].astype(BF16)
 
     blocks = width // block
+    up.second()
+    linear_sum(3)
+    raw_ref[:, own, :] = lmine[pl.ds(at.y * chunk, chunk)]
     compression(0, blocks // 3)
-    up.second()
+    for copy in ycopies:
+        copy.wait()
+
+    @pl.loop(0, chunk)
+    def _(n):
+        out, term, grad = norm(raw_ref[n].astype(F32), lcot_ref[n].astype(F32), gain)
+        out_ref[n] = out.astype(BF16)
+        rsum[...] += term
+        glc[n] = grad.astype(BF16)
+
+    mid = pl.ds(zbase + at.y * chunk, chunk)
+    gather_ref[mid] = glc[:, own, :]
+    zcopies = [send(gather_ref.at[mid], gather_ref.at[mid], zsems, 0, zpeer)]
+    gcopies = []
+    for k in (1, 2, 3):
+        y, peer = at.to_y(k)
+        gcopies.append(send(glc.at[:, rows(y, step), :], gather_ref.at[mid], ysems, k - 1, peer))
+    rmine[n_bias : n_bias + 1, :width] = column_sums(rsum[...])
+    rcopies = [send(rmine, rgot.at[k - 1], rsems, k - 1, at.to_y(k)[1]) for k in (1, 2, 3)]
+    compression(blocks // 3, 2 * blocks // 3)
     for k in (1, 2, 3):
         gcopies[k - 1].wait()
         source = lax.rem(at.y + 4 - k, 4)
-        there = pl.ds(zbase + source * out_fields, out_fields)
+        there = pl.ds(zbase + source * chunk, chunk)
         zcopies.append(send(gather_ref.at[there], gather_ref.at[there], zsems, k, zpeer))
     for copy in rcopies:
         copy.wait()
-    rmine[...] = (rmine[...] + rgot[1]) + (rgot[0] + rgot[2])
-    rcopy = send(rmine, rother, rsems, 3, zpeer)
-    compression(blocks // 3, blocks)
+    rtotal[...] = (rmine[...] + rgot[1]) + (rgot[0] + rgot[2])
+    rcopy = send(rtotal, rother, rsems, 3, zpeer)
+    compression(2 * blocks // 3, blocks)
     ccopies = []
     for k in (1, 2, 3):
         y, peer = at.to_y(k)
         ccopies.append(send(cb.at[rows(y, step)], cgot.at[k - 1], csems, k - 1, peer))
+    down.last()
     for copy in ccopies:
         copy.wait()
     cmine[...] = (
-        cb[own_part].astype(F32)
-        + cgot[0].astype(F32)
-        + cgot[1].astype(F32)
-        + cgot[2].astype(F32)
+        cb[own].astype(F32) + cgot[0].astype(F32) + cgot[1].astype(F32) + cgot[2].astype(F32)
     ).astype(BF16)
     ccopy = send(cmine, cother, csems, 3, zpeer)
     up.third()
     rcopy.wait()
-    rows_out[...] = rmine[...] + rother[...]
+    rows_out[...] = rtotal[...] + rother[...]
     ccopy.wait()
     gcomp_ref[...] = ((cmine[...].astype(F32) + cother[...].astype(F32)) * scale).astype(BF16)
     up.last()
@@ -649,6 +650,7 @@
         ],
         0,
         80,
+        16,
         comp_part,
         w_linear,
         turned,
@@ -660,93 +662,65 @@
         "feb,fn->neb", spread, wl_all.reshape(4 * fields, 128)[:, :nl], preferred_element_type=F32
     ).astype(BF16)
     columns = cot_first.shape[0] * width
-    fm_out, gain_fm, grad_pre, bias_part, lc_raw, grad_down = call(
-        middle_kernel,
+    extra_shape = (8, 256)
+    n_bias, n_extra, slab = units // 256, 8, 16
+    fm_out, lc_out, gathered, grad_comp, grad_down, grad_up, extra = call(
+        back_kernel,
         [
             (cot_first.shape, BF16),
-            ((width, examples), F32),
-            ((units, examples), BF16),
-            ((quarter, 1), F32),
             (cot_second.shape, BF16),
+            ((nl, part, examples), BF16),
+            ((part, kk, examples), BF16),
             ((own_rows, columns), F32),
+            ((own_rows, fields * kk), F32),
+            (extra_shape, F32),
         ],
-        [VMEM(cot_first.shape, BF16)]
+        [VMEM(cot_first.shape, BF16), VMEM((units, examples), BF16)]
         + row_scratch
         + [
             VMEM((nl // 2, part, examples), BF16),
             VMEM((nl // 2, part, examples), BF16),
+            VMEM(cot_second.shape, BF16),
+            VMEM(cot_second.shape, BF16),
             VMEM((16, 2, own_rows, columns), BF16),
+            VMEM((16, 2, own_rows, fields * kk), BF16),
         ]
         + stages(columns)
+        + stages(fields * kk)
         + [
+            VMEM((fields, kk, examples), F32),
+            VMEM((fields, slab, examples), F32),
+            VMEM((width, kk, examples), BF16),
+            VMEM((3, part, kk, examples), BF16),
+            VMEM((part, kk, examples), BF16),
+            VMEM((part, kk, examples), BF16),
+            VMEM((width, examples), F32),
+            VMEM(extra_shape, F32),
+            VMEM((3,) + extra_shape, F32),
+            VMEM(extra_shape, F32),
+            VMEM(extra_shape, F32),
             pltpu.SemaphoreType.DMA((2, 7)),
             pltpu.SemaphoreType.DMA((2, 7)),
+            pltpu.SemaphoreType.DMA((2, 3)),
+            pltpu.SemaphoreType.DMA((2, 4)),
+            pltpu.SemaphoreType.DMA((2, 4)),
             pltpu.SemaphoreType.DMA((2, 7)),
+            pltpu.SemaphoreType.DMA((2, 7)),
+            pltpu.SemaphoreType.DMA((2, 4)),
         ],
         1,
-        35,
+        80,
+        28,
         hidden,
         hidden_pre,
         w_down,
         cot_first,
         gain,
         lin,
-    )
-    flat = flat.reshape(fields * kk, examples)
-    up_part = jnp.einsum("hb,jb->hj", grad_pre, flat, preferred_element_type=F32).astype(BF16)
-    grad_inter = (
-        jnp.einsum("hj,hb->jb", w_up, grad_pre, preferred_element_type=F32)
-        .astype(BF16)
-        .reshape(fields, kk, examples)
-    )
-    n_bias = units // 256
-    y = lax.rem(lax.axis_index("field"), 4)
-    bias_rows = lax.dynamic_update_slice_in_dim(
-        jnp.zeros((units,), F32), 0.5 * bias_part.reshape(-1), y * quarter, axis=0
-    ).reshape(n_bias, 256)
-    gain_row = jnp.pad(jnp.sum(gain_fm, axis=1), (0, 256 - width)).reshape(1, 256)
-    extra = jnp.pad(jnp.concatenate([bias_rows, gain_row]), ((0, 3), (0, 0)))
-
-    out_fields, n_extra, slab = nl // 8, extra.shape[0], 16
-    lc_out, gathered, grad_comp, grad_up, extra = call(
-        grads_kernel,
-        [
-            (cot_second.shape, BF16),
-            ((nl, part, examples), BF16),
-            ((part, kk, examples), BF16),
-            ((own_rows, fields * kk), F32),
-            (extra.shape, F32),
-        ],
-        [
-            VMEM((fields, kk, examples), F32),
-            VMEM((fields, slab, examples), F32),
-            VMEM((width, kk, examples), BF16),
-            VMEM((3, part, kk, examples), BF16),
-            VMEM((part, kk, examples), BF16),
-            VMEM((part, kk, examples), BF16),
-            VMEM(cot_second.shape, BF16),
-        ]
-        + stages(fields * kk)
-        + [
-            VMEM((3,) + extra.shape, F32),
-            VMEM(extra.shape, F32),
-            VMEM((width, examples), F32),
-            VMEM(extra.shape, F32),
-            pltpu.SemaphoreType.DMA((2, 3)),
-            pltpu.SemaphoreType.DMA((2, 4)),
-            pltpu.SemaphoreType.DMA((2, 4)),
-            pltpu.SemaphoreType.DMA((2, 7)),
-            pltpu.SemaphoreType.DMA((2, 4)),
-        ],
-        2,
-        45,
-        lc_raw,
-        up_part.reshape(16, 2, own_rows, fields * kk),
-        grad_inter,
+        flat,
+        w_up,
         turned,
         cot_second,
-        gain,
-        extra,
     )
     mixed = jnp.concatenate(
         [
@@ -770,8 +744,9 @@
             VMEM((3, total_rows, 128), BF16),
             pltpu.SemaphoreType.DMA((2, 10)),
         ],
-        3,
+        2,
         15,
+        8,
         mixed,
         extra,
     )

time: 234 us -> 213 us (0.910)
  local copies, waits for them, and re-layouts: 21 us -> 9.72 us
  matrix products: 16.7 us -> 9.19 us
    unnamed x54 -> x28, local copies, waits for them, and re-layouts: 18.2 us -> 8.41 us
    dot_general x2 -> x0, matrix products: 5.03 us -> none  [the longest x1 3.63 us: local(): jnp.einsum('hb,jb->hj', grad_pre, flat, preferred_element_type=F32)]
    dot_general x1, matrix products: 4.02 us -> 1.53 us  [local(): jnp.einsum('feb,neb->fn', spread, gathered, preferred_element_type=F32)]
    pallas_call x4 -> x3, Pallas kernels: 194 us -> 193 us  [call(): pl.pallas_call(kernel, out_shape=[jax.ShapeDtypeStruct(shape, dtype) for...]
where the time goes in v3:
time: 213 us
  Pallas kernels  193 us (91%)
  local copies, waits for them, and re-layouts  9.72 us (5%)
  matrix products  9.19 us (4%)
    pallas_call x3, Pallas kernels, call(): pl.pallas_call(kernel, out_shape=[jax.ShapeDtypeStruct(shape, dtype) for...  193 us
    unnamed x28, local copies, waits for them, and re-layouts  8.41 us
    dot_general x1, matrix products, local(): jnp.einsum('feb,fk->ekb', turned, compress, preferred_element_type=F32)  5.33 us

profile of v3, /device:TPU:1, one launch (start us, length us, event | category | flops | bytes accessed | tf_op | source)
XLA Modules:
  0.0 212.8 jit_solution(3114962495730350262)
XLA Ops:
  0.7 0.6 copy-done
  1.3 5.3 %fusion.11.part_ref = bf16[192,16,128]{2,1,0:T(8,128)(2,1)S(1)} fusion(bf16[96,192,128]{2,1,0:T(8,128)(2,1)} %bitcast.28, bf16[96,16]{0,1:T(8,128)(2,1)S(1)} %copy-done), kind=kOutput, calls=%fused_computation.10 | convolution fusion | flops 75890688 | bytes 5508096 | tf_op jit(solution)/shard_map/feb,fk->ekb/dot_general | solution.py:610
  6.7 1.9 copy-done.2
  8.6 89.0 %shard_map.152 = (bf16[4,96,128]{2,1,0:T(8,128)(2,1)S(1)}, bf16[4,96,48,128]{3,2,1,0:T(8,128)(2,1)S(1)}, bf16[96,16,128]{2,1,0:T(8,128)(2,1)S(1)}, bf16[1024,128]{1,0:T(8,128)(2,1)S(1)}, f32[256,128]{1,0:T(8,128)S(1)}) custom-call(bf16[192,16,128]{2,1,0:T(8,128)(2,1)S(1)} %fusion.11.part_ref, bf16[96,96]{1,0:T(8,128)(2,1)S(1)} %copy-done.7, ...), custom_call_target="tpu_custom_call" | custom-call | bytes 240000000 | tf_op jit(solution)/shard_map/pallas_call | solution.py:89
  97.6 1.0 fusion.6
  98.6 0.5 copy.48.lin_ref
  99.2 0.3 copy-done.3
  99.4 0.7 copy-done.4
  100.2 0.1 copy-done.5
  100.3 86.3 %shard_map.153 = (bf16[6,192,128]{2,1,0:T(8,128)(2,1)S(1)}, bf16[12,192,128]{2,1,0:T(8,128)(2,1)S(1)}, bf16[96,48,128]{2,1,0:T(8,128)(2,1)S(1)}, bf16[48,16,128]...) custom-call(bf16[1024,128]{1,0:T(8,128)(2,1)S(1)} %get-tuple-element.23.hidden_ref, ...), custom_call_target="tpu_custom_call" | custom-call | bytes 240000000 | tf_op jit(solution)/shard_map/pallas_call | solution.py:89
  186.7 1.5 fusion.15
  188.2 1.3 fusion.20
  189.5 0.1 pad.2.clone
  189.6 0.1 maximum_maximum_fusion
  189.7 0.1 copy.24
  189.9 17.6 %shard_map.154 = (f32[96,96]{1,0:T(8,128)S(1)}, f32[16,96]{1,0:T(8,128)S(1)}, f32[8,256]{1,0:T(8,128)S(1)}) custom-call(f32[4,96,128]{2,1,0:T(8,128)S(1)} %bitcast.34, f32[8,256]{1,0:T(8,128)S(1)} %get-tuple-element.32.rows_ref), custom_call_target="tpu_custom_call" | custom-call | bytes 45000000 | tf_op jit(solution)/shard_map/pallas_call | solution.py:89
  207.5 0.6 copy.26
  208.1 0.6 slice.11
  208.7 0.7 copy.55
  209.4 0.8 copy.56
  210.2 0.6 copy.57
  210.8 0.7 copy.58
  211.5 0.7 copy.59
  212.1 0.6 copy.60
  (18 shorter events, 0.2 us)
Async XLA Ops:
  0.6 0.7 copy-start
  0.6 6.0 %copy-start.1 = (bf16[128,96,192]{0,2,1:T(8,128)(2,1)S(1)}, bf16[128,96,192]{0,2,1:T(8,128)(2,1)}, u32[]{:S(2)}) copy-start(bf16[128,96,192]{0,2,1:T(8,128)(2,1)} %param.9) | copy-start | bytes 14155780
  0.7 6.0 %copy-start.8 = (f32[1024]{0:T(1024)S(1)}, f32[1024]{0:T(1024)}, u32[]{:S(2)}) copy-start(f32[1024]{0:T(1024)} %param.12) | copy-start | bytes 12292
  0.7 6.0 %copy-start.7 = (bf16[96,96]{1,0:T(8,128)(2,1)S(1)}, bf16[96,96]{1,0:T(8,128)(2,1)}, u32[]{:S(2)}) copy-start(bf16[96,96]{1,0:T(8,128)(2,1)} %wl_ref.1) | copy-start | bytes 55300
  6.7 1.9 copy-start.2
  97.5 1.5 copy-start.9
  97.6 1.9 copy-start.3
  97.6 2.6 %copy-start.4 = (bf16[1024,1152]{1,0:T(8,128)(2,1)S(1)}, bf16[1024,1152]{1,0:T(8,128)(2,1)}, u32[]{:S(2)}) copy-start(bf16[1024,1152]{1,0:T(8,128)(2,1)} %down_ref.1) | copy-start | bytes 7077892
  97.6 2.7 %copy-start.5 = (bf16[128,12,192]{0,2,1:T(8,128)(2,1)S(1)}, bf16[128,12,192]{0,2,1:T(8,128)(2,1)}, u32[]{:S(2)}) copy-start(bf16[128,12,192]{0,2,1:T(8,128)(2,1)} %param.17) | copy-start | bytes 1769476
  97.6 2.7 %copy-start.6 = (bf16[128,6,192]{0,2,1:T(8,128)(2,1)S(1)}, bf16[128,6,192]{0,2,1:T(8,128)(2,1)}, u32[]{:S(2)}) copy-start(bf16[128,6,192]{0,2,1:T(8,128)(2,1)} %param.16) | copy-start | bytes 884740

commit v4 on v3

--- a/solution.py
+++ b/solution.py
@@ -101,26 +101,6 @@
     return pl.ds(pl.multiple_of(start * size, size), size)
 
 
-def field_sum(at, part_ref, got, mine, other, sems, between):
-    step = part_ref.shape[0] // 4
-    copies = []
-    for k in (1, 2, 3):
-        y, peer = at.to_y(k)
-        copies.append(send(part_ref.at[rows(y, step)], got.at[k - 1], sems, k - 1, peer))
-    for copy in copies:
-        copy.wait()
-    mine[...] = (
-        part_ref[rows(at.y, step)].astype(F32)
-        + got[0].astype(F32)
-        + got[1].astype(F32)
-        + got[2].astype(F32)
-    ).astype(BF16)
-    copy = send(mine, other, sems, 3, at.to_zh()[1])
-    between()
-    copy.wait()
-    return mine[...].astype(F32) + other[...].astype(F32)
-
-
 def gather_rows(at, out_ref, sems):
     own = rows(at.y, out_ref.shape[0] // 4)
     return [send(out_ref.at[own], out_ref.at[own], sems, 3 + k, at.to_y(k)[1]) for k in (1, 2, 3)]
@@ -137,128 +117,6 @@
     dn = cot * gain
     grad = rstd * (dn - mean0(dn) - normed * mean0(dn * normed))
     return normed * gain, cot * normed, grad
-
-
-def front_kernel(
-    pieces,
-    part_ref,
-    wl_ref,
-    emb_ref,
-    up_ref,
-    bias_ref,
-    wl_out,
-    emb_out,
-    flat_ref,
-    hidden_ref,
-    pre_ref,
-    cgot,
-    cmine,
-    cother,
-    comp,
-    compf,
-    embf,
-    part,
-    got,
-    mine,
-    other,
-    csems,
-    wsems,
-    esems,
-    psems,
-):
-    at = Place()
-    fields, width, examples = emb_ref.shape
-    step, kk = width // 4, part_ref.shape[1]
-    scale = float(width) ** (-0.5)
-    block = embf.shape[0]
-    size = fields // pieces
-    background = []
-
-    def piece(p):
-        here = pl.ds(p * size, size)
-        for k in (1, 2, 3):
-            y, peer = at.to_y(k)
-            background.append(
-                send(emb_ref.at[here, rows(y, step), :], emb_out.at[k, here], esems, p * 3 + k - 1, peer)
-            )
-
-    def own_part():
-        wl_out[0] = jnp.zeros(wl_out.shape[1:], BF16)
-        wl_out[0, :, : wl_ref.shape[1]] = wl_ref[...]
-        emb_out[0] = emb_ref[:, rows(at.y, step), :]
-
-    greet(at.field_group(), own_part)
-    copies = []
-    for k in (1, 2, 3):
-        y, peer = at.to_y(k)
-        copies.append(send(part_ref.at[rows(y, step)], cgot.at[k - 1], csems, k - 1, peer))
-    for k in (1, 2, 3):
-        background.append(send(wl_out.at[0], wl_out.at[k], wsems, k - 1, at.to_y(k)[1]))
-    for copy in copies:
-        copy.wait()
-    cmine[...] = (
-        part_ref[rows(at.y, step)].astype(F32)
-        + cgot[0].astype(F32)
-        + cgot[1].astype(F32)
-        + cgot[2].astype(F32)
-    ).astype(BF16)
-    copy = send(cmine, cother, csems, 3, at.to_zh()[1])
-    piece(0)
-    piece(1)
-    copy.wait()
-    own = rows(at.y, step)
-    comp[own] = (cmine[...].astype(F32) + cother[...].astype(F32)).astype(BF16)
-    copies = [send(comp.at[own], comp.at[own], csems, 3 + k, at.to_y(k)[1]) for k in (1, 2, 3)]
-    for copy in copies:
-        copy.wait()
-    compf[...] = comp[...].astype(F32)
-
-    def interact(start, stop):
-        @pl.loop(start, stop)
-        def _(i):
-            embf[...] = emb_ref[pl.ds(i * block, block)].astype(F32)
-
-            def terms(e, totals):
-                c = compf[e]
-                return tuple(t + c * embf[j, pl.ds(e, 1), :] for j, t in enumerate(totals))
-
-            totals = lax.fori_loop(
-                0, width, terms, tuple(jnp.zeros((kk, examples), F32) for _ in range(block)), unroll=8
-            )
-            for j in range(block):
-                flat_ref[i * block + j] = (totals[j] * scale).astype(BF16)
-
-    blocks = fields // block
-    cuts = [blocks * p // 3 for p in range(4)]
-    for p in range(3):
-        piece(2 + p)
-        interact(cuts[p], cuts[p + 1])
-
-    flat = flat_ref[...].reshape(fields * kk, examples)
-    units = up_ref.shape[0]
-    quarter = units // 4
-
-    @pl.loop(0, 4)
-    def _(r):
-        part[rows(r, quarter)] = jnp.dot(
-            up_ref[rows(r, quarter), :], flat, preferred_element_type=F32
-        ).astype(BF16)
-
-    def after(p):
-        def go():
-            if p < pieces:
-                piece(p)
-
-        return go
-
-    bias = jnp.transpose(jnp.broadcast_to(bias_ref[:, rows(at.y, quarter)], (examples, quarter)))
-    pre = field_sum(at, part, got, mine, other, psems, after(5)) + bias
-    pre_ref[...] = pre
-    hidden_ref[rows(at.y, quarter)] = (pre / (1.0 + jnp.exp(-pre))).astype(BF16)
-    for copy in gather_rows(at, hidden_ref, psems):
-        copy.wait()
-    for copy in background:
-        copy.wait()
 
 
 class BatchSum:
@@ -308,17 +166,18 @@
         self.out[...] = total
 
 
-def back_kernel(
-    hidden_ref,
-    pre_ref,
+def layer_kernel(
+    pieces,
+    part_ref,
+    wl_ref,
+    emb_ref,
+    up_ref,
+    bias_ref,
     down_ref,
     cot_ref,
     gain_ref,
-    lin_ref,
-    flat_ref,
-    up_ref,
-    emb_ref,
     lcot_ref,
+    emb_out,
     fm_ref,
     out_ref,
     gather_ref,
@@ -326,12 +185,29 @@
     down_out,
     up_out,
     rows_out,
-    gfm_ref,
-    gpre_ref,
+    wl_out,
+    flat_ref,
+    hidden_ref,
+    pre_ref,
+    comp,
+    compf,
+    ccgot,
+    ccmine,
+    ccother,
+    embi,
+    embx,
+    linf,
+    lin_ref,
     part,
     got,
     mine,
     other,
+    gfm_ref,
+    gpre_ref,
+    hpart,
+    hgot,
+    hmine,
+    hother,
     lmine,
     lother,
     raw_ref,
@@ -355,6 +231,10 @@
     rgot,
     rtotal,
     rother,
+    ccsems,
+    wsems,
+    esems,
+    psems,
     hsems,
     lsems,
     ysems,
@@ -365,23 +245,181 @@
     rsems,
 ):
     at = Place()
-    units, examples = hidden_ref.shape
-    fields, width = emb_ref.shape[:2]
-    quarter, step, kk = units // 4, width // 4, flat_ref.shape[1]
+    fields, width, examples = emb_ref.shape
+    step, kk = width // 4, part_ref.shape[1]
     scale = float(width) ** (-0.5)
+    block = embi.shape[0]
+    slab = embx.shape[0] // (4 * fields)
+    background = []
+    moved = []
+
+    def piece(p):
+        here = pl.ds(p % 2 * (fields // 2), fields // 2)
+        for k in (1, 2, 3):
+            y, peer = at.to_y(k)
+            there = pl.ds(pl.multiple_of(y * step + p // 2 * slab, slab), slab)
+            moved.append(
+                send(
+                    emb_ref.at[here, there, :],
+                    emb_out.at[k, here, pl.ds(p // 2 * slab, slab), :],
+                    esems,
+                    p * 3 + k - 1,
+                    peer,
+                )
+            )
+
+    def own_part():
+        wl_out[0] = jnp.zeros(wl_out.shape[1:], BF16)
+        wl_out[0, :, : wl_ref.shape[1]] = wl_ref[...]
+        emb_out[0] = emb_ref[:, rows(at.y, step), :]
+
+    greet(at.field_group() + at.batch_group(), own_part)
+    copies = []
+    for k in (1, 2, 3):
+        y, peer = at.to_y(k)
+        copies.append(send(part_ref.at[rows(y, step)], ccgot.at[k - 1], ccsems, k - 1, peer))
+    for k in (1, 2, 3):
+        background.append(send(wl_out.at[0], wl_out.at[k], wsems, k - 1, at.to_y(k)[1]))
+    for copy in copies:
+        copy.wait()
+    ccmine[...] = (
+        part_ref[rows(at.y, step)].astype(F32)
+        + ccgot[0].astype(F32)
+        + ccgot[1].astype(F32)
+        + ccgot[2].astype(F32)
+    ).astype(BF16)
+    copy = send(ccmine, ccother, ccsems, 3, at.to_zh()[1])
+    piece(0)
+    piece(1)
+    copy.wait()
+    own = rows(at.y, step)
+    comp[own] = (ccmine[...].astype(F32) + ccother[...].astype(F32)).astype(BF16)
+    copies = [send(comp.at[own], comp.at[own], ccsems, 3 + k, at.to_y(k)[1]) for k in (1, 2, 3)]
+    for copy in copies:
+        copy.wait()
+    compf[...] = comp[...].astype(F32)
+
+    def interact(start, stop):
+        @pl.loop(start, stop)
+        def _(i):
+            embi[...] = emb_ref[pl.ds(i * block, block)].astype(F32)
+
+            def terms(e, totals):
+                c = compf[e]
+                return tuple(t + c * embi[j, pl.ds(e, 1), :] for j, t in enumerate(totals))
+
+            totals = lax.fori_loop(
+                0, width, terms, tuple(jnp.zeros((kk, examples), F32) for _ in range(block)), unroll=8
+            )
+            for j in range(block):
+                flat_ref[i * block + j] = (totals[j] * scale).astype(BF16)
+
+    blocks = fields // block
+    cuts = [blocks * p // 3 for p in range(4)]
+    for p in range(3):
+        if p < 2:
+            piece(2 + p)
+        interact(cuts[p], cuts[p + 1])
+
+    flat = flat_ref[...].reshape(fields * kk, examples)
+    units = up_ref.shape[0]
+    quarter = units // 4
+
+    @pl.loop(0, 4)
+    def _(r):
+        part[rows(r, quarter)] = jnp.dot(
+            up_ref[rows(r, quarter), :], flat, preferred_element_type=F32
+        ).astype(BF16)
+
+    bias = jnp.transpose(jnp.broadcast_to(bias_ref[:, rows(at.y, quarter)], (examples, quarter)))
+    copies = []
+    for k in (1, 2, 3):
+        y, peer = at.to_y(k)
+        copies.append(send(part.at[rows(y, quarter)], got.at[k - 1], psems, k - 1, peer))
+
+    for copy in background:
+        copy.wait()
+    wt = jnp.transpose(wl_out[...].reshape(4 * fields, wl_out.shape[2]).astype(F32))
+    wt = wt[: lin_ref.shape[0]].astype(BF16)
+    n_lin = lin_ref.shape[0]
+    zh, zpeer = at.to_zh()
+    lcopies = []
+
+    def linear(g):
+        for copy in moved[6 * g : 6 * g + 6]:
+            copy.wait()
+        for k in range(4):
+
+            @pl.loop(0, fields // 8)
+            def _(i):
+                embx[rows(k * (fields // 8) + i, 8 * slab), :] = (
+                    emb_out[k, pl.ds(i * 8, 8), g * slab : (g + 1) * slab, :]
+                    .astype(F32)
+                    .reshape(8 * slab, examples)
+                )
+
+        for e in range(slab):
+            linf[pl.ds(e, n_lin, stride=slab), :] = jnp.dot(
+                wt,
+                embx[pl.ds(e, 4 * fields, stride=slab), :].astype(BF16),
+                preferred_element_type=F32,
+            )
+        here = slice(g * slab, (g + 1) * slab)
+        lin_ref[:, here, :] = linf[...].reshape(n_lin, slab, examples).astype(BF16)
+        lcopies.append(
+            send(
+                lin_ref.at[pl.ds(zh * (n_lin // 2), n_lin // 2), here, :],
+                lother.at[:, here, :],
+                lsems,
+                g,
+                zpeer,
+            )
+        )
+
+    linear(0)
+    for copy in copies:
+        copy.wait()
+    mine[...] = (
+        part[rows(at.y, quarter)].astype(F32)
+        + got[0].astype(F32)
+        + got[1].astype(F32)
+        + got[2].astype(F32)
+    ).astype(BF16)
+    copy = send(mine, other, psems, 3, zpeer)
+    piece(4)
+    linear(1)
+    copy.wait()
+    pre = mine[...].astype(F32) + other[...].astype(F32) + bias
+    pre_ref[...] = pre
+    hidden_ref[rows(at.y, quarter)] = (pre / (1.0 + jnp.exp(-pre))).astype(BF16)
+    for copy in gather_rows(at, hidden_ref, psems):
+        copy.wait()
     chunk = raw_ref.shape[0]
     half = 4 * chunk
-    zh, zpeer = at.to_zh()
     zbase = at.zh * half
     own = rows(at.y, step)
     gain = gain_ref[...]
-    lcopies = []
-
-    def linear(j):
-        field = lax.rem(at.y + 1 + j, 4) * chunk
-        lcopies.append(
-            send(lin_ref.at[pl.ds(zh * half + field, chunk)], lother.at[pl.ds(field, chunk)], lsems, j, zpeer)
-        )
+    ycopies = []
+
+    def linear_sum(g):
+        lcopies[g].wait()
+        here = slice(g * slab, (g + 1) * slab)
+        there = pl.ds(pl.multiple_of(at.y * step + g * slab, slab), slab)
+        lmine[:, here, :] = (
+            lin_ref[pl.ds(zbase, half), here, :].astype(F32) + lother[:, here, :].astype(F32)
+        ).astype(BF16)
+        for k in (1, 2, 3):
+            y, peer = at.to_y(k)
+            ycopies.append(
+                send(
+                    lmine.at[pl.ds(y * chunk, chunk), here, :],
+                    raw_ref.at[:, there, :],
+                    lsems,
+                    3 + g * 3 + k - 1,
+                    peer,
+                )
+            )
+        raw_ref[:, there, :] = lmine[pl.ds(at.y * chunk, chunk), here, :]
 
     def column_sums(values):
         return jnp.sum(jnp.transpose(values), axis=0, keepdims=True)
@@ -405,21 +443,21 @@
                 gfm_ref[n + m] = grad.astype(BF16)
         rsum[...] = gain_total
 
-    greet(at.field_group() + at.batch_group(), forward)
-    linear(0)
-    linear(1)
+    piece(5)
+    linear_sum(0)
+    forward()
     gfm = gfm_ref[...].reshape(down_ref.shape[1], examples)
 
     @pl.loop(0, 4)
     def _(r):
-        part[rows(r, quarter)] = jnp.dot(
+        hpart[rows(r, quarter)] = jnp.dot(
             down_ref[rows(r, quarter), :], gfm, preferred_element_type=F32
         ).astype(BF16)
 
     copies = []
     for k in (1, 2, 3):
         y, peer = at.to_y(k)
-        copies.append(send(part.at[rows(y, quarter)], got.at[k - 1], hsems, k - 1, peer))
+        copies.append(send(hpart.at[rows(y, quarter)], hgot.at[k - 1], hsems, k - 1, peer))
 
     def weights(left_ref, right, into):
         @pl.loop(0, 4)
@@ -435,41 +473,27 @@
     weights(hidden_ref, gfm, dpart)
     down = BatchSum(at, dpart, d1, d2, d3, dsems, down_out)
     down.first()
+    linear_sum(1)
     for copy in copies:
         copy.wait()
-    mine[...] = (
-        part[rows(at.y, quarter)].astype(F32)
-        + got[0].astype(F32)
-        + got[1].astype(F32)
-        + got[2].astype(F32)
+    hmine[...] = (
+        hpart[rows(at.y, quarter)].astype(F32)
+        + hgot[0].astype(F32)
+        + hgot[1].astype(F32)
+        + hgot[2].astype(F32)
     ).astype(BF16)
-    copy = send(mine, other, hsems, 3, zpeer)
+    copy = send(hmine, hother, hsems, 3, zpeer)
     linear(2)
-    linear(3)
     down.second()
     pre = pre_ref[...]
     sigma = 1.0 / (1.0 + jnp.exp(-pre))
     slope = sigma * (1.0 + pre * (1.0 - sigma))
     copy.wait()
-    grad = (mine[...].astype(F32) + other[...].astype(F32)) * slope
+    grad = (hmine[...].astype(F32) + hother[...].astype(F32)) * slope
     gpre_ref[rows(at.y, quarter)] = grad.astype(BF16)
     copies = gather_rows(at, gpre_ref, hsems)
     rmine[pl.ds(at.y, 1), :] = 0.5 * column_sums(grad)
-    ycopies = []
-
-    def linear_sum(j):
-        lcopies[j].wait()
-        field, peer = at.to_y(j + 1)
-        for n in range(chunk):
-            lmine[field * chunk + n] = (
-                lin_ref[zbase + field * chunk + n].astype(F32) + lother[field * chunk + n].astype(F32)
-            ).astype(BF16)
-        if j < 3:
-            ycopies.append(
-                send(lmine.at[pl.ds(field * chunk, chunk)], raw_ref.at[:, own, :], lsems, 4 + j, peer)
-            )
-
-    linear_sum(0)
+    linear_sum(2)
     for copy in copies:
         copy.wait()
     flat = flat_ref[...].reshape(fields * kk, examples)
@@ -477,18 +501,7 @@
     weights(gpre_ref, flat, upart)
     up = BatchSum(at, upart, u1, u2, u3, usems, up_out)
     up.first()
-    linear_sum(1)
-
-    @pl.loop(0, 6)
-    def _(r):
-        size = fields * kk // 6
-        block = lax.dot_general(
-            up_ref[:, rows(r, size)], gpre, (((0,), (0,)), ((), ())), preferred_element_type=F32
-        ).astype(BF16)
-        interf[rows(r, fields // 6)] = block.astype(F32).reshape(fields // 6, kk, examples)
-
-    linear_sum(2)
-    down.third()
+
     block = embf.shape[1]
 
     def compression(start, stop):
@@ -507,10 +520,6 @@
                 cb[i * block + j] = totals[j].astype(BF16)
 
     blocks = width // block
-    up.second()
-    linear_sum(3)
-    raw_ref[:, own, :] = lmine[pl.ds(at.y * chunk, chunk)]
-    compression(0, blocks // 3)
     for copy in ycopies:
         copy.wait()
 
@@ -530,7 +539,17 @@
         gcopies.append(send(glc.at[:, rows(y, step), :], gather_ref.at[mid], ysems, k - 1, peer))
     rmine[n_bias : n_bias + 1, :width] = column_sums(rsum[...])
     rcopies = [send(rmine, rgot.at[k - 1], rsems, k - 1, at.to_y(k)[1]) for k in (1, 2, 3)]
-    compression(blocks // 3, 2 * blocks // 3)
+    @pl.loop(0, 6)
+    def _(r):
+        size = fields * kk // 6
+        block = lax.dot_general(
+            up_ref[:, rows(r, size)], gpre, (((0,), (0,)), ((), ())), preferred_element_type=F32
+        ).astype(BF16)
+        interf[rows(r, fields // 6)] = block.astype(F32).reshape(fields // 6, kk, examples)
+
+    up.second()
+    down.third()
+    compression(0, blocks // 3)
     for k in (1, 2, 3):
         gcopies[k - 1].wait()
         source = lax.rem(at.y + 4 - k, 4)
@@ -540,19 +559,19 @@
         copy.wait()
     rtotal[...] = (rmine[...] + rgot[1]) + (rgot[0] + rgot[2])
     rcopy = send(rtotal, rother, rsems, 3, zpeer)
-    compression(2 * blocks // 3, blocks)
+    compression(blocks // 3, blocks)
     ccopies = []
     for k in (1, 2, 3):
         y, peer = at.to_y(k)
         ccopies.append(send(cb.at[rows(y, step)], cgot.at[k - 1], csems, k - 1, peer))
-    down.last()
+    up.third()
     for copy in ccopies:
         copy.wait()
     cmine[...] = (
         cb[own].astype(F32) + cgot[0].astype(F32) + cgot[1].astype(F32) + cgot[2].astype(F32)
     ).astype(BF16)
     ccopy = send(cmine, cother, csems, 3, zpeer)
-    up.third()
+    down.last()
     rcopy.wait()
     rows_out[...] = rtotal[...] + rother[...]
     ccopy.wait()
@@ -624,49 +643,13 @@
         VMEM((quarter, examples), BF16),
         VMEM((quarter, examples), BF16),
     ]
-    wl_all, spread, flat, hidden, hidden_pre = call(
-        functools.partial(front_kernel, pieces),
-        [
-            ((4, fields, 128), BF16),
-            ((4, fields, part, examples), BF16),
-            ((fields, kk, examples), BF16),
-            ((units, examples), BF16),
-            ((quarter, examples), F32),
-        ],
-        [
-            VMEM((3, part, kk, examples), BF16),
-            VMEM((part, kk, examples), BF16),
-            VMEM((part, kk, examples), BF16),
-            VMEM((width, kk, examples), BF16),
-            VMEM((width, kk, examples), F32),
-            VMEM((block, width, examples), F32),
-        ]
-        + row_scratch
-        + [
-            pltpu.SemaphoreType.DMA((2, 7)),
-            pltpu.SemaphoreType.DMA((2, 3)),
-            pltpu.SemaphoreType.DMA((2, 3 * pieces)),
-            pltpu.SemaphoreType.DMA((2, 7)),
-        ],
-        0,
-        80,
-        16,
-        comp_part,
-        w_linear,
-        turned,
-        w_up,
-        up_bias.reshape(1, -1),
-    )
-    spread = spread.reshape(4 * fields, part, examples)
-    lin = jnp.einsum(
-        "feb,fn->neb", spread, wl_all.reshape(4 * fields, 128)[:, :nl], preferred_element_type=F32
-    ).astype(BF16)
     columns = cot_first.shape[0] * width
     extra_shape = (8, 256)
     n_bias, n_extra, slab = units // 256, 8, 16
-    fm_out, lc_out, gathered, grad_comp, grad_down, grad_up, extra = call(
-        back_kernel,
+    spread, fm_out, lc_out, gathered, grad_comp, grad_down, grad_up, extra = call(
+        functools.partial(layer_kernel, pieces),
         [
+            ((4, fields, part, examples), BF16),
             (cot_first.shape, BF16),
             (cot_second.shape, BF16),
             ((nl, part, examples), BF16),
@@ -675,7 +658,23 @@
             ((own_rows, fields * kk), F32),
             (extra_shape, F32),
         ],
-        [VMEM(cot_first.shape, BF16), VMEM((units, examples), BF16)]
+        [
+            VMEM((4, fields, 128), BF16),
+            VMEM((fields, kk, examples), BF16),
+            VMEM((units, examples), BF16),
+            VMEM((quarter, examples), F32),
+            VMEM((width, kk, examples), BF16),
+            VMEM((width, kk, examples), F32),
+            VMEM((3, part, kk, examples), BF16),
+            VMEM((part, kk, examples), BF16),
+            VMEM((part, kk, examples), BF16),
+            VMEM((block, width, examples), F32),
+            VMEM((4 * fields * slab, examples), F32),
+            VMEM((nl * slab, examples), F32),
+            VMEM((nl, part, examples), BF16),
+        ]
+        + row_scratch
+        + [VMEM(cot_first.shape, BF16), VMEM((units, examples), BF16)]
         + row_scratch
         + [
             VMEM((nl // 2, part, examples), BF16),
@@ -700,7 +699,11 @@
             VMEM(extra_shape, F32),
             VMEM(extra_shape, F32),
             pltpu.SemaphoreType.DMA((2, 7)),
+            pltpu.SemaphoreType.DMA((2, 3)),
+            pltpu.SemaphoreType.DMA((2, 3 * pieces)),
             pltpu.SemaphoreType.DMA((2, 7)),
+            pltpu.SemaphoreType.DMA((2, 7)),
+            pltpu.SemaphoreType.DMA((2, 12)),
             pltpu.SemaphoreType.DMA((2, 3)),
             pltpu.SemaphoreType.DMA((2, 4)),
             pltpu.SemaphoreType.DMA((2, 4)),
@@ -708,20 +711,20 @@
             pltpu.SemaphoreType.DMA((2, 7)),
             pltpu.SemaphoreType.DMA((2, 4)),
         ],
-        1,
-        80,
-        28,
-        hidden,
-        hidden_pre,
+        0,
+        140,
+        36,
+        comp_part,
+        w_linear,
+        turned,
+        w_up,
+        up_bias.reshape(1, -1),
         w_down,
         cot_first,
         gain,
-        lin,
-        flat,
-        w_up,
-        turned,
         cot_second,
     )
+    spread = spread.reshape(4 * fields, part, examples)
     mixed = jnp.concatenate(
         [
             jnp.einsum("feb,neb->fn", spread, gathered, preferred_element_type=F32),
@@ -744,7 +747,7 @@
             VMEM((3, total_rows, 128), BF16),
             pltpu.SemaphoreType.DMA((2, 10)),
         ],
-        2,
+        1,
         15,
         8,
         mixed,

time: 213 us -> 201 us (0.944)
  Pallas kernels: 193 us -> 184 us
    pallas_call x3 -> x2, Pallas kernels: 193 us -> 184 us  [call(): pl.pallas_call(kernel, out_shape=[jax.ShapeDtypeStruct(shape, dtype) for...]
    unnamed x28 -> x24, local copies, waits for them, and re-layouts: 8.41 us -> 7.36 us
where the time goes in v4:
time: 201 us
  Pallas kernels  184 us (92%)
  local copies, waits for them, and re-layouts  8.21 us (4%)
  matrix products  8.19 us (4%)
    pallas_call x2, Pallas kernels, call(): pl.pallas_call(kernel, out_shape=[jax.ShapeDtypeStruct(shape, dtype) for...  184 us
    unnamed x24, local copies, waits for them, and re-layouts  7.36 us
    dot_general x1, matrix products, local(): jnp.einsum('feb,fk->ekb', turned, compress, preferred_element_type=F32)  5.33 us

profile of v4, /device:TPU:1, one launch (start us, length us, event | category | flops | bytes accessed | tf_op | source)
XLA Modules:
  0.0 201.1 jit_solution(1646895567538540592)
XLA Ops:
  0.6 0.0 copy-start
  0.7 0.0 copy-start.7
  0.7 0.0 copy-start.6
  0.7 0.6 copy-done
  1.3 5.3 %fusion.9.part_ref = bf16[192,16,128]{2,1,0:T(8,128)(2,1)S(1)} fusion(bf16[96,192,128]{2,1,0:T(8,128)(2,1)} %bitcast.32, bf16[96,16]{0,1:T(8,128)(2,1)S(1)} %copy-done), kind=kOutput, calls=%fused_computation.7 | convolution fusion | flops 75890688 | bytes 5508096 | tf_op jit(solution)/shard_map/feb,fk->ekb/dot_general | solution.py:629
  6.7 0.1 broadcast_in_dim.8.gain_ref
  6.8 0.0 copy-start.3
  6.8 1.1 copy-done.3
  7.9 1.0 copy-done.4
  8.8 166.8 %shard_map.152 = (bf16[4,96,48,128]{3,2,1,0:T(8,128)(2,1)S(1)}, bf16[6,192,128]{2,1,0:T(8,128)(2,1)S(1)}, bf16[12,192,128]{2,1,0:T(8,128)(2,1)S(1)}, bf16[96,48,...) custom-call(bf16[192,16,128]{2,1,0:T(8,128)(2,1)S(1)} %fusion.9.part, ...), custom_call_target="tpu_custom_call" | custom-call | bytes 420000000 | tf_op jit(solution)/shard_map/pallas_call | solution.py:89
  175.7 1.5 fusion.13
  177.2 1.3 fusion.18
  178.5 0.1 pad.2.clone
  178.6 0.1 maximum_maximum_fusion
  178.7 0.1 copy.21
  178.8 17.0 %shard_map.153 = (f32[96,96]{1,0:T(8,128)S(1)}, f32[16,96]{1,0:T(8,128)S(1)}, f32[8,256]{1,0:T(8,128)S(1)}) custom-call(f32[4,96,128]{2,1,0:T(8,128)S(1)} %bitcast.23, f32[8,256]{1,0:T(8,128)S(1)} %get-tuple-element.24.rows_ref), custom_call_target="tpu_custom_call" | custom-call | bytes 45000000 | tf_op jit(solution)/shard_map/pallas_call | solution.py:89
  195.9 0.6 copy.22
  196.5 0.6 slice.7
  197.0 0.7 copy.47
  197.8 0.8 copy.48
  198.6 0.6 copy.49
  199.2 0.7 copy.50
  199.9 0.7 copy.51
  200.5 0.6 copy.52
  (11 shorter events, 0.0 us)
Async XLA Ops:
  0.6 0.7 copy-start
  0.7 6.0 %copy-start.7 = (f32[192]{0:T(256)S(1)}, f32[192]{0:T(256)}, u32[]{:S(2)}) copy-start(f32[192]{0:T(256)} %param.15) | copy-start | bytes 2308
  0.7 6.1 %copy-start.6 = (f32[1024]{0:T(1024)S(1)}, f32[1024]{0:T(1024)}, u32[]{:S(2)}) copy-start(f32[1024]{0:T(1024)} %param.12) | copy-start | bytes 12292
  0.7 6.1 %copy-start.1 = (bf16[1024,1536]{1,0:T(8,128)(2,1)S(1)}, bf16[1024,1536]{1,0:T(8,128)(2,1)}, u32[]{:S(2)}) copy-start(bf16[1024,1536]{1,0:T(8,128)(2,1)} %up_ref.1) | copy-start | bytes 9437188
  0.7 6.1 %copy-start.2 = (bf16[1024,1152]{1,0:T(8,128)(2,1)S(1)}, bf16[1024,1152]{1,0:T(8,128)(2,1)}, u32[]{:S(2)}) copy-start(bf16[1024,1152]{1,0:T(8,128)(2,1)} %down_ref.1) | copy-start | bytes 7077892
  0.7 6.1 %copy-start.5 = (bf16[96,96]{1,0:T(8,128)(2,1)S(1)}, bf16[96,96]{1,0:T(8,128)(2,1)}, u32[]{:S(2)}) copy-start(bf16[96,96]{1,0:T(8,128)(2,1)} %wl_ref.1) | copy-start | bytes 55300
  6.8 1.1 copy-start.3
  7.9 1.0 copy-start.4

commit v5 on v4

--- a/solution.py
+++ b/solution.py
@@ -498,15 +498,21 @@
         copy.wait()
     flat = flat_ref[...].reshape(fields * kk, examples)
     gpre = gpre_ref[...]
-    weights(gpre_ref, flat, upart)
-    up = BatchSum(at, upart, u1, u2, u3, usems, up_out)
-    up.first()
+    @pl.loop(0, 6)
+    def _(r):
+        size = fields * kk // 6
+        block = lax.dot_general(
+            up_ref[:, rows(r, size)], gpre, (((0,), (0,)), ((), ())), preferred_element_type=F32
+        ).astype(BF16)
+        interf[rows(r, fields // 6)] = block.astype(F32).reshape(fields // 6, kk, examples)
+
 
     block = embf.shape[1]
 
-    def compression(start, stop):
-        @pl.loop(start, stop)
-        def _(i):
+    def compression(y):
+        @pl.loop(0, step // block)
+        def _(r):
+            i = y * (step // block) + r
             embf[...] = emb_ref[:, rows(i, block), :].astype(F32)
 
             def terms(f, totals):
@@ -519,7 +525,6 @@
             for j in range(block):
                 cb[i * block + j] = totals[j].astype(BF16)
 
-    blocks = width // block
     for copy in ycopies:
         copy.wait()
 
@@ -539,17 +544,20 @@
         gcopies.append(send(glc.at[:, rows(y, step), :], gather_ref.at[mid], ysems, k - 1, peer))
     rmine[n_bias : n_bias + 1, :width] = column_sums(rsum[...])
     rcopies = [send(rmine, rgot.at[k - 1], rsems, k - 1, at.to_y(k)[1]) for k in (1, 2, 3)]
-    @pl.loop(0, 6)
-    def _(r):
-        size = fields * kk // 6
-        block = lax.dot_general(
-            up_ref[:, rows(r, size)], gpre, (((0,), (0,)), ((), ())), preferred_element_type=F32
-        ).astype(BF16)
-        interf[rows(r, fields // 6)] = block.astype(F32).reshape(fields // 6, kk, examples)
-
+
+    weights(gpre_ref, flat, upart)
+    up = BatchSum(at, upart, u1, u2, u3, usems, up_out)
+    up.first()
+    down.third()
+    ccopies = []
+
+    def compression_to(k):
+        y, peer = at.to_y(k)
+        compression(y)
+        ccopies.append(send(cb.at[rows(y, step)], cgot.at[k - 1], csems, k - 1, peer))
+
+    compression_to(1)
     up.second()
-    down.third()
-    compression(0, blocks // 3)
     for k in (1, 2, 3):
         gcopies[k - 1].wait()
         source = lax.rem(at.y + 4 - k, 4)
@@ -559,11 +567,9 @@
         copy.wait()
     rtotal[...] = (rmine[...] + rgot[1]) + (rgot[0] + rgot[2])
     rcopy = send(rtotal, rother, rsems, 3, zpeer)
-    compression(blocks // 3, blocks)
-    ccopies = []
-    for k in (1, 2, 3):
-        y, peer = at.to_y(k)
-        ccopies.append(send(cb.at[rows(y, step)], cgot.at[k - 1], csems, k - 1, peer))
+    compression_to(2)
+    compression_to(3)
+    compression(at.y)
     up.third()
     for copy in ccopies:
         copy.wait()

time: 201 us -> 200 us (level)
  no operation moved by 1% of the time
where the time goes in v5:
time: 200 us
  Pallas kernels  183 us (92%)
  local copies, waits for them, and re-layouts  8.21 us (4%)
  matrix products  8.2 us (4%)
    pallas_call x2, Pallas kernels, call(): pl.pallas_call(kernel, out_shape=[jax.ShapeDtypeStruct(shape, dtype) for...  183 us
    unnamed x24, local copies, waits for them, and re-layouts  7.36 us
    dot_general x1, matrix products, local(): jnp.einsum('feb,fk->ekb', turned, compress, preferred_element_type=F32)  5.33 us

profile of v5, /device:TPU:1, one launch (start us, length us, event | category | flops | bytes accessed | tf_op | source)
XLA Modules:
  0.0 200.3 jit_solution(11766163610433904060)
XLA Ops:
  0.6 0.0 copy-start
  0.7 0.0 copy-start.7
  0.7 0.0 copy-start.6
  0.7 0.6 copy-done
  1.3 5.3 %fusion.9.part_ref = bf16[192,16,128]{2,1,0:T(8,128)(2,1)S(1)} fusion(bf16[96,192,128]{2,1,0:T(8,128)(2,1)} %bitcast.32, bf16[96,16]{0,1:T(8,128)(2,1)S(1)} %copy-done), kind=kOutput, calls=%fused_computation.7 | convolution fusion | flops 75890688 | bytes 5508096 | tf_op jit(solution)/shard_map/feb,fk->ekb/dot_general | solution.py:635
  6.7 0.1 broadcast_in_dim.8.gain_ref
  6.8 0.0 copy-start.3
  6.8 1.1 copy-done.3
  7.9 1.0 copy-done.4
  8.8 166.8 %shard_map.152 = (bf16[4,96,48,128]{3,2,1,0:T(8,128)(2,1)S(1)}, bf16[6,192,128]{2,1,0:T(8,128)(2,1)S(1)}, bf16[12,192,128]{2,1,0:T(8,128)(2,1)S(1)}, bf16[96,48,...) custom-call(bf16[192,16,128]{2,1,0:T(8,128)(2,1)S(1)} %fusion.9.part, ...), custom_call_target="tpu_custom_call" | custom-call | bytes 420000000 | tf_op jit(solution)/shard_map/pallas_call | solution.py:89
  175.6 1.5 fusion.13
  177.1 1.3 fusion.18
  178.5 0.1 pad.2.clone
  178.6 0.1 maximum_maximum_fusion
  178.7 0.1 copy.21
  178.8 16.2 %shard_map.153 = (f32[96,96]{1,0:T(8,128)S(1)}, f32[16,96]{1,0:T(8,128)S(1)}, f32[8,256]{1,0:T(8,128)S(1)}) custom-call(f32[4,96,128]{2,1,0:T(8,128)S(1)} %bitcast.23, f32[8,256]{1,0:T(8,128)S(1)} %get-tuple-element.24.rows_ref), custom_call_target="tpu_custom_call" | custom-call | bytes 45000000 | tf_op jit(solution)/shard_map/pallas_call | solution.py:89
  195.0 0.6 copy.22
  195.6 0.6 slice.7
  196.2 0.7 copy.47
  196.9 0.8 copy.48
  197.7 0.6 copy.49
  198.3 0.7 copy.50
  199.0 0.7 copy.51
  199.7 0.6 copy.52
  (11 shorter events, 0.0 us)
Async XLA Ops:
  0.6 0.7 copy-start
  0.7 6.0 %copy-start.7 = (f32[192]{0:T(256)S(1)}, f32[192]{0:T(256)}, u32[]{:S(2)}) copy-start(f32[192]{0:T(256)} %param.15) | copy-start | bytes 2308
  0.7 6.1 %copy-start.6 = (f32[1024]{0:T(1024)S(1)}, f32[1024]{0:T(1024)}, u32[]{:S(2)}) copy-start(f32[1024]{0:T(1024)} %param.12) | copy-start | bytes 12292
  0.7 6.1 %copy-start.1 = (bf16[1024,1536]{1,0:T(8,128)(2,1)S(1)}, bf16[1024,1536]{1,0:T(8,128)(2,1)}, u32[]{:S(2)}) copy-start(bf16[1024,1536]{1,0:T(8,128)(2,1)} %up_ref.1) | copy-start | bytes 9437188
  0.7 6.1 %copy-start.2 = (bf16[1024,1152]{1,0:T(8,128)(2,1)S(1)}, bf16[1024,1152]{1,0:T(8,128)(2,1)}, u32[]{:S(2)}) copy-start(bf16[1024,1152]{1,0:T(8,128)(2,1)} %down_ref.1) | copy-start | bytes 7077892
  0.7 6.1 %copy-start.5 = (bf16[96,96]{1,0:T(8,128)(2,1)S(1)}, bf16[96,96]{1,0:T(8,128)(2,1)}, u32[]{:S(2)}) copy-start(bf16[96,96]{1,0:T(8,128)(2,1)} %wl_ref.1) | copy-start | bytes 55300
  6.8 1.1 copy-start.3
  7.9 1.0 copy-start.4
